TPU v7x, 32 devices: a whole 2x2x4 slice. The times are simulated.
32 devices in a mesh: batch: 8 (over z, x), task: 4 (over y, core).
Axes of the slice: x: 2, y: 2, z: 4, core: 2. Of those that a mesh axis runs over, the one named last changes fastest.
Arguments:
- tokens: bfloat16 [2, 32, 1024, 1024], P(None, ('batch', 'task')), may hold values from -6 to 6
- cotangent: bfloat16 [2, 32, 1024, 1024], P(None, ('batch', 'task')), may hold values from -6 to 6
- segment_ids: int32 [2, 32, 1024], P(None, ('batch', 'task')), may hold values from 0 to 15, never falling along the last dimension, each value on 1 to 128 neighbouring positions
- task_ids: int32 [2, 32, 16], P(None, ('batch', 'task')), may hold values from 0 to 3
- ln1_gain: bfloat16 [1024], replicated, may hold values from 0.5 to 1.5
- ln1_bias: bfloat16 [1024], replicated, may hold values from -1.75 to 1.75
- w_qkv: bfloat16 [1024, 3072], replicated, may hold values from -0.1875 to 0.1875
- b_qkv: bfloat16 [3072], replicated, may hold values from -1.75 to 1.75
- w_attn_out: bfloat16 [1024, 1024], replicated, may hold values from -0.5 to 0.5
- b_attn_out: bfloat16 [1024], replicated, may hold values from -1.75 to 1.75
- ln2_gain: bfloat16 [1024], replicated, may hold values from 0.5 to 1.5
- ln2_bias: bfloat16 [1024], replicated, may hold values from -1.75 to 1.75
- w_fc: bfloat16 [1024, 4096], replicated, may hold values from -0.1875 to 0.1875
- b_fc: bfloat16 [4096], replicated, may hold values from -1.75 to 1.75
- w_proj: bfloat16 [4096, 1024], replicated, may hold values from -0.09375 to 0.09375
- b_proj: bfloat16 [1024], replicated, may hold values from -1.75 to 1.75
- prefix_embed: bfloat16 [4, 10, 1024], P('task'), may hold values from -6 to 6
- reparam_in: bfloat16 [4, 1024, 512], P('task'), may hold values from -0.1875 to 0.1875
- reparam_in_bias: bfloat16 [4, 512], P('task'), may hold values from -3 to 3
- reparam_out: bfloat16 [4, 512, 2048], P('task'), may hold values from -0.25 to 0.25
- reparam_out_bias: bfloat16 [4, 2048], P('task'), may hold values from -3 to 3
Outputs:
- block_out: bfloat16 [2, 32, 1024, 1024], P(None, ('batch', 'task'))
- input_grad: bfloat16 [2, 32, 1024, 1024], P(None, ('batch', 'task'))
- grad_prefix_embed: float32 [4, 10, 1024], P('task')
- grad_reparam_in: float32 [4, 1024, 512], P('task')
- grad_reparam_in_bias: float32 [4, 512], P('task')
- grad_reparam_out: float32 [4, 512, 2048], P('task')
- grad_reparam_out_bias: float32 [4, 2048], P('task')
Inputs may be any that keep to these rules, and one draw needn't show every extreme that they name: `segment_ids`: in each row segment numbers never fall and each example holds 1 to 128 tokens; some example holds exactly 128.
All inputs are finite; a program needn't handle non-finite values.
Results may differ from a plain program's by a relative error of at most 0.02.
Values may be sent and summed in bfloat16 or wider, within the bound.
A program may use at most 448 MiB of HBM per device.

v0:
```python
import jax
import jax.numpy as jnp
from jax import lax
from jax.sharding import PartitionSpec as P

HEADS = 16
QB = 512
MOST = 128


epsilon = 1e-05
negative = -1e30


def layer_norm(hidden, gain, shift):
    center = jnp.mean(hidden, axis=-1, keepdims=True)
    centred = hidden - center
    spread = jnp.mean(centred * centred, axis=-1, keepdims=True)
    return centred * lax.rsqrt(spread + epsilon) * gain + shift


def gelu_tanh(values):
    return (
        0.5
        * values
        * (1.0 + jnp.tanh(0.7978845608028654 * (values + 0.044715 * values * values * values)))
    )


def contract_last(left, right):
    return lax.dot_general(
        left, right, (((1,), (1,)), ((), ())), preferred_element_type=jnp.float32
    )


def prefix_forward(embed, weight_in, bias_in, weight_out, bias_out):
    pre_hidden = (
        jnp.einsum("tpd,tdr->tpr", embed, weight_in, preferred_element_type=jnp.float32)
        + bias_in.astype(jnp.float32)[:, None, :]
    )
    hidden = jnp.tanh(pre_hidden)
    states = jnp.einsum(
        "tpr,tre->tpe", hidden.astype(jnp.bfloat16), weight_out, preferred_element_type=jnp.float32
    )
    states = (states + bias_out.astype(jnp.float32)[:, None, :]).astype(jnp.bfloat16)
    return (hidden, states)


def prefix_backward(embed, weight_in, weight_out, hidden, summed_states):
    grad_states = summed_states.astype(jnp.bfloat16)
    rounded = hidden.astype(jnp.bfloat16)
    grad_weight_out = jnp.einsum(
        "tpr,tpe->tre", rounded, grad_states, preferred_element_type=jnp.float32
    )
    grad_bias_out = jnp.sum(grad_states.astype(jnp.float32), axis=1)
    grad_hidden = jnp.einsum(
        "tpe,tre->tpr", grad_states, weight_out, preferred_element_type=jnp.float32
    )
    grad_pre = (grad_hidden * (1.0 - hidden * hidden)).astype(jnp.bfloat16)
    grad_weight_in = jnp.einsum("tpd,tpr->tdr", embed, grad_pre, preferred_element_type=jnp.float32)
    grad_bias_in = jnp.sum(grad_pre.astype(jnp.float32), axis=1)
    grad_embed = jnp.einsum("tpr,tdr->tpd", grad_pre, weight_in, preferred_element_type=jnp.float32)
    return (grad_embed, grad_weight_in, grad_bias_in, grad_weight_out, grad_bias_out)


def block_scores(queries, keys_all, prefix_keys, segments, task_mask, start, key_start, scale):
    block_end = start + QB
    query_block = queries[start:block_end]
    own_scores = (
        jnp.einsum(
            "qhd,khd->hqk",
            query_block,
            keys_all[key_start:block_end],
            preferred_element_type=jnp.float32,
        )
        * scale
    )
    prefix_scores = (
        jnp.einsum("qhd,khd->hqk", query_block, prefix_keys, preferred_element_type=jnp.float32)
        * scale
    )
    query_pos = jnp.arange(start, block_end)
    key_pos = jnp.arange(key_start, block_end)
    own_mask = (segments[start:block_end, None] == segments[None, key_start:block_end]) & (
        key_pos[None, :] <= query_pos[:, None]
    )
    own_scores = jnp.where(own_mask[None], own_scores, negative)
    prefix_scores = jnp.where(task_mask[None, start:block_end], prefix_scores, negative)
    return (own_scores, prefix_scores)


def row_pass(row, grad_out, segments, row_tasks, states, weights):
    (
        gain_one,
        shift_one,
        w_qkv,
        b_qkv,
        w_attn,
        b_attn,
        gain_two,
        shift_two,
        w_fc,
        b_fc,
        w_proj,
        b_proj,
    ) = weights
    seq_len, width = row.shape
    head_dim = width // HEADS
    scale = head_dim ** (-0.5)
    tasks_all = states.shape[0]
    prefix_len = states.shape[1]
    row_wide = row.astype(jnp.float32)
    normed = layer_norm(row_wide, gain_one, shift_one).astype(jnp.bfloat16)
    mixed = (jnp.dot(normed, w_qkv, preferred_element_type=jnp.float32) + b_qkv).astype(
        jnp.bfloat16
    )
    queries = mixed[:, :width].reshape(seq_len, HEADS, head_dim)
    keys_all = mixed[:, width : 2 * width].reshape(seq_len, HEADS, head_dim)
    values_all = mixed[:, 2 * width :].reshape(seq_len, HEADS, head_dim)
    prefix_keys = states[:, :, :width].reshape(tasks_all * prefix_len, HEADS, head_dim)
    prefix_values = states[:, :, width:].reshape(tasks_all * prefix_len, HEADS, head_dim)
    segment_match = segments[:, None] == jnp.arange(row_tasks.shape[0])[None, :]
    token_task = jnp.sum(jnp.where(segment_match, row_tasks[None, :], 0), axis=1)
    task_mask = jnp.repeat(
        token_task[:, None] == jnp.arange(tasks_all)[None, :], prefix_len, axis=1
    )
    starts = [(start, max(start - MOST, 0)) for start in range(0, seq_len, QB)]
    attended_blocks = []
    log_totals = []
    for start, key_start in starts:
        own_scores, prefix_scores = block_scores(
            queries, keys_all, prefix_keys, segments, task_mask, start, key_start, scale
        )
        row_max = jnp.maximum(jnp.max(own_scores, axis=2), jnp.max(prefix_scores, axis=2))[
            ..., None
        ]
        own_exp = jnp.exp(own_scores - row_max)
        prefix_exp = jnp.exp(prefix_scores - row_max)
        totals = jnp.sum(own_exp, axis=2, keepdims=True) + jnp.sum(
            prefix_exp, axis=2, keepdims=True
        )
        log_totals.append(row_max + jnp.log(totals))
        own_probs = (own_exp / totals).astype(jnp.bfloat16)
        prefix_probs = (prefix_exp / totals).astype(jnp.bfloat16)
        block_out = jnp.einsum(
            "hqk,khd->qhd",
            own_probs,
            values_all[key_start : start + QB],
            preferred_element_type=jnp.float32,
        )
        block_out = block_out + jnp.einsum(
            "hqk,khd->qhd", prefix_probs, prefix_values, preferred_element_type=jnp.float32
        )
        attended_blocks.append(block_out)
    attended = jnp.concatenate(attended_blocks, axis=0).reshape(seq_len, width).astype(jnp.bfloat16)
    resid = row_wide + jnp.dot(attended, w_attn, preferred_element_type=jnp.float32) + b_attn
    normed_two = layer_norm(resid, gain_two, shift_two).astype(jnp.bfloat16)
    pre_act = jnp.dot(normed_two, w_fc, preferred_element_type=jnp.float32) + b_fc
    activation = gelu_tanh(pre_act).astype(jnp.bfloat16)
    result = (
        resid + jnp.dot(activation, w_proj, preferred_element_type=jnp.float32) + b_proj
    ).astype(jnp.bfloat16)
    grad_act = contract_last(grad_out, w_proj)
    grad_pre = jax.vjp(gelu_tanh, pre_act)[1](grad_act)[0].astype(jnp.bfloat16)
    grad_normed_two = contract_last(grad_pre, w_fc)
    norm_two_pull = jax.vjp(lambda hidden: layer_norm(hidden, gain_two, shift_two), resid)[1]
    grad_resid = grad_out.astype(jnp.float32) + norm_two_pull(grad_normed_two)[0]
    grad_attended = contract_last(grad_resid.astype(jnp.bfloat16), w_attn).astype(jnp.bfloat16)
    grad_heads = grad_attended.reshape(seq_len, HEADS, head_dim)
    grad_query_blocks = []
    grad_keys = jnp.zeros((seq_len, HEADS, head_dim), jnp.float32)
    grad_values = jnp.zeros((seq_len, HEADS, head_dim), jnp.float32)
    grad_prefix_keys = jnp.zeros(prefix_keys.shape, jnp.float32)
    grad_prefix_values = jnp.zeros(prefix_values.shape, jnp.float32)
    for (start, key_start), log_total in zip(starts, log_totals):
        block_end = start + QB
        own_scores, prefix_scores = block_scores(
            queries, keys_all, prefix_keys, segments, task_mask, start, key_start, scale
        )
        own_probs = jnp.exp(own_scores - log_total)
        prefix_probs = jnp.exp(prefix_scores - log_total)
        grad_block = grad_heads[start:block_end]
        value_window = values_all[key_start:block_end]
        own_dprobs = jnp.einsum(
            "qhd,khd->hqk", grad_block, value_window, preferred_element_type=jnp.float32
        )
        prefix_dprobs = jnp.einsum(
            "qhd,khd->hqk", grad_block, prefix_values, preferred_element_type=jnp.float32
        )
        delta = jnp.sum(own_probs * own_dprobs, axis=2, keepdims=True) + jnp.sum(
            prefix_probs * prefix_dprobs, axis=2, keepdims=True
        )
        own_grad = (own_probs * (own_dprobs - delta)).astype(jnp.bfloat16)
        prefix_grad = (prefix_probs * (prefix_dprobs - delta)).astype(jnp.bfloat16)
        query_block = queries[start:block_end]
        grad_query = jnp.einsum(
            "hqk,khd->qhd",
            own_grad,
            keys_all[key_start:block_end],
            preferred_element_type=jnp.float32,
        )
        grad_query = grad_query + jnp.einsum(
            "hqk,khd->qhd", prefix_grad, prefix_keys, preferred_element_type=jnp.float32
        )
        grad_query_blocks.append(grad_query * scale)
        grad_keys = grad_keys.at[key_start:block_end].add(
            jnp.einsum("hqk,qhd->khd", own_grad, query_block, preferred_element_type=jnp.float32)
            * scale
        )
        grad_prefix_keys = (
            grad_prefix_keys
            + jnp.einsum(
                "hqk,qhd->khd", prefix_grad, query_block, preferred_element_type=jnp.float32
            )
            * scale
        )
        grad_values = grad_values.at[key_start:block_end].add(
            jnp.einsum(
                "hqk,qhd->khd",
                own_probs.astype(jnp.bfloat16),
                grad_block,
                preferred_element_type=jnp.float32,
            )
        )
        grad_prefix_values = grad_prefix_values + jnp.einsum(
            "hqk,qhd->khd",
            prefix_probs.astype(jnp.bfloat16),
            grad_block,
            preferred_element_type=jnp.float32,
        )
    grad_mixed = jnp.concatenate(
        [
            jnp.concatenate(grad_query_blocks, axis=0).reshape(seq_len, width),
            grad_keys.reshape(seq_len, width),
            grad_values.reshape(seq_len, width),
        ],
        axis=1,
    ).astype(jnp.bfloat16)
    grad_normed = contract_last(grad_mixed, w_qkv)
    norm_one_pull = jax.vjp(lambda hidden: layer_norm(hidden, gain_one, shift_one), row_wide)[1]
    grad_row = (grad_resid + norm_one_pull(grad_normed)[0]).astype(jnp.bfloat16)
    grad_states = jnp.concatenate(
        [
            grad_prefix_keys.reshape(tasks_all, prefix_len, width),
            grad_prefix_values.reshape(tasks_all, prefix_len, width),
        ],
        axis=2,
    )
    return (result, grad_row, grad_states)


def on_device(
    tokens,
    cotangent,
    segment_ids,
    task_ids,
    ln1_gain,
    ln1_bias,
    w_qkv,
    b_qkv,
    w_attn_out,
    b_attn_out,
    ln2_gain,
    ln2_bias,
    w_fc,
    b_fc,
    w_proj,
    b_proj,
    prefix_embed,
    reparam_in,
    reparam_in_bias,
    reparam_out,
    reparam_out_bias,
):
    hidden, own_states = prefix_forward(
        prefix_embed, reparam_in, reparam_in_bias, reparam_out, reparam_out_bias
    )
    states = lax.all_gather(own_states, "task", axis=0, tiled=True)
    weights = (
        ln1_gain.astype(jnp.float32),
        ln1_bias.astype(jnp.float32),
        w_qkv,
        b_qkv.astype(jnp.float32),
        w_attn_out,
        b_attn_out.astype(jnp.float32),
        ln2_gain.astype(jnp.float32),
        ln2_bias.astype(jnp.float32),
        w_fc,
        b_fc.astype(jnp.float32),
        w_proj,
        b_proj.astype(jnp.float32),
    )
    micro_count, rows_local = (tokens.shape[0], tokens.shape[1])
    results = []
    input_rows = []
    grad_states = jnp.zeros(states.shape, jnp.float32)
    for micro_index in range(micro_count):
        result, grad_row, row_states = row_pass(
            tokens[micro_index, 0],
            cotangent[micro_index, 0],
            segment_ids[micro_index, 0],
            task_ids[micro_index, 0],
            states,
            weights,
        )
        results.append(result)
        input_rows.append(grad_row)
        grad_states = grad_states + row_states
    block_out = jnp.stack(results, axis=0).reshape(tokens.shape)
    input_grad = jnp.stack(input_rows, axis=0).reshape(tokens.shape)
    everything = lax.psum(grad_states.astype(jnp.bfloat16), "batch")
    summed = lax.psum_scatter(everything, "task", scatter_dimension=0, tiled=True).astype(
        jnp.float32
    )
    grads = prefix_backward(prefix_embed, reparam_in, reparam_out, hidden, summed)
    return (block_out, input_grad, grads[0], grads[1], grads[2], grads[3], grads[4])


def solution(mesh):
    in_specs = (
        P(None, ("batch", "task"), None, None),
        P(None, ("batch", "task"), None, None),
        P(None, ("batch", "task"), None),
        P(None, ("batch", "task"), None),
        P(),
        P(),
        P(),
        P(),
        P(),
        P(),
        P(),
        P(),
        P(),
        P(),
        P(),
        P(),
        P("task", None, None),
        P("task", None, None),
        P("task", None),
        P("task", None, None),
        P("task", None),
    )
    out_specs = (
        P(None, ("batch", "task"), None, None),
        P(None, ("batch", "task"), None, None),
        P("task", None, None),
        P("task", None, None),
        P("task", None),
        P("task", None, None),
        P("task", None),
    )
    return jax.shard_map(
        on_device, mesh=mesh, in_specs=in_specs, out_specs=out_specs, check_vma=False
    )
```

profile of v0, /device:TPU:0, one launch (start us, length us, event | category | flops | bytes accessed | tf_op | source)
XLA Modules:
  0.0 764.2 jit_solution(8235557278937838391)
XLA Ops:
  27.5 10.3 %add_convert_fusion = bf16[1024,3072]{1,0:T(8,128)(2,1)S(1)} fusion(f32[3072]{0:T(1024)S(1)} %convert_element_type.212, bf16[1024,3072]{1,0:T(8,128)(2,1)} %param.43, bf16[1,1,1024,1024]{2,3,1,0:T(8,128)(2,1)S(1)} %copy-done.5, f32[1024]{0:T(1024)S(1)} %fusion.235, f32[1024]{0:T(1024)S(1)} %get-tuple-element.233, f32[1024]{0:T(1024)S(1)} %convert_element_type.210, ...), kind=kOutput, calls=%fused_computation.54 | convolution fusion | flops 6455033856 | bytes 14708736 | tf_op jit(solution)/shard_map/dot_general | solution.py:114
  66.5 18.6 %all-gather.1 = bf16[4,10,2048]{2,1,0:T(8,128)(2,1)S(1)} all-gather(bf16[1,10,2048]{2,1,0:T(8,128)(2,1)S(1)} %fusion.85), channel_id=2, replica_groups=mesh['batch'=8,'task'=4] {'task'}, dimensions={0}, use_global_device_ids=true | all-gather | bytes 204800 | tf_op jit(solution)/shard_map/all_gather | solution.py:278
  131.8 9.6 %fusion.27 = f32[16,64,512]{2,1,0:T(8,128)S(1)} fusion(bf16[640,16,64]{0,2,1:T(8,128)(2,1)S(1)} %bitcast.370, f32[16,512,640]{2,1,0:T(8,128)} %copy-done.1, f32[16,512]{1,0:T(8,128)S(1)} %get-tuple-element.140, f32[16,512]{1,0:T(8,128)S(1)} %max.43), kind=kOutput, calls=%fused_computation.61 | convolution fusion | flops 686817280 | bytes 24444928 | tf_op jit(solution)/shard_map/hqk,khd->qhd/dot_general | solution.py:145
  183.3 9.7 %fusion.26 = f32[16,64,512]{2,1,0:T(8,128)S(1)} fusion(bf16[640,16,64]{0,2,1:T(8,128)(2,1)} %bitcast.372, f32[16,512,640]{2,1,0:T(8,128)} %copy-done.2, f32[16,512]{1,0:T(8,128)S(1)} %get-tuple-element.146, f32[16,512]{1,0:T(8,128)S(1)} %max.41), kind=kOutput, calls=%fused_computation.60 | convolution fusion | flops 686817280 | bytes 24444928 | tf_op jit(solution)/shard_map/hqk,khd->qhd/dot_general | solution.py:145
  201.4 9.2 %fusion.281 = (f32[16,512]{1,0:T(8,128)S(1)}, f32[16,512,512]{1,2,0:T(8,128)}) fusion(bf16[512,16,64]{0,2,1:T(8,128)(2,1)S(1)} %bitcast.343, bf16[512,16,64]{0,2,1:T(8,128)(2,1)} %bitcast.364, pred[512,512]{0,1:T(8,128)(4,1)} %fusion.181), kind=kOutput, calls=%fused_computation.388 | convolution fusion | flops 549445632 | bytes 19169280 | tf_op jit(solution)/shard_map/qhd,khd->hqk/dot_general | solution.py:70
  235.9 12.9 %fusion.92 = f32[1024,4096]{1,0:T(8,128)} fusion(bf16[1024,4096]{1,0:T(8,128)(2,1)S(1)} %bitcast.397, f32[1024,1024]{0,1:T(8,128)S(1)} %copy-done.46, f32[1024]{0:T(1024)S(1)} %copy-done.139, f32[1024]{0:T(1024)S(1)} %broadcast_multiply_fusion, f32[1024]{0:T(1024)S(1)} %copy-done.150, f32[1024]{0:T(1024)S(1)} %copy-done.141), kind=kOutput, calls=%fused_computation.148 | convolution fusion | flops 8595177472 | bytes 29376512 | tf_op jit(solution)/shard_map/dot_general | solution.py:158
  248.7 12.7 %fusion.90 = f32[1024,4096]{1,0:T(8,128)} fusion(bf16[1024,4096]{1,0:T(8,128)(2,1)S(1)} %bitcast.397, f32[1024,1024]{0,1:T(8,128)S(1)} %get-tuple-element.210, f32[1024]{0:T(1024)S(1)} %copy-done.150, f32[1024]{0:T(1024)S(1)} %copy-done.141, f32[1024]{0:T(1024)S(1)} %fusion.234, f32[1024]{0:T(1024)S(1)} %broadcast_multiply_fusion.2), kind=kOutput, calls=%fused_computation.146 | convolution fusion | flops 8595177472 | bytes 29376512 | tf_op jit(solution)/shard_map/dot_general | solution.py:158
  263.9 32.3 %fusion.38 = f32[1024,1024]{0,1:T(8,128)} fusion(bf16[1024,4096]{1,0:T(8,128)(2,1)} %param.49, f32[1024,4096]{1,0:T(8,128)} %fusion.92, f32[4096]{0:T(1024)S(1)} %copy-done.137, bf16[4096,1024]{1,0:T(8,128)(2,1)} %param.51, bf16[2,1,1024,1024]{3,2,1,0:T(8,128)(2,1)} %param.38), kind=kOutput, calls=%fused_computation.70 | convolution fusion | flops 17284726784 | bytes 39862272 | tf_op jit(solution)/shard_map/dot_general | solution.py:31
  296.2 35.7 %multiply_reduce_fusion.5 = (f32[1024]{0:T(1024)S(1)}, f32[1024]{0:T(1024)S(1)}, f32[1024,1024]{0,1:T(8,128)}) fusion(f32[1024,1024]{0,1:T(8,128)} %copy-done.47, f32[1024]{0:T(1024)S(1)} %copy-done.141, f32[1024]{0:T(1024)S(1)} %broadcast_multiply_fusion.2, f32[1024,1024]{0,1:T(8,128)} %fusion.38, f32[1024,1024]{0,1:T(8,128)} %copy-done.45, ...), kind=kOutput, calls=%fused_computation.123 | convolution fusion | flops 17293115392 | bytes 52465664 | tf_op jit(solution)/shard_map/dot_general | solution.py:31
  348.7 12.0 %multiply_reduce_fusion.2 = (f32[16,512]{1,0:T(8,128)}, f32[16,512,512]{1,2,0:T(8,128)}) fusion(f32[16,512,512]{1,2,0:T(8,128)} %get-tuple-element.196, f32[16,512]{1,0:T(8,128)S(1)} %copy-done.93, bf16[512,16,64]{0,2,1:T(8,128)(2,1)S(1)} %bitcast.346, bf16[512,16,64]{0,2,1:T(8,128)(2,1)S(1)} %bitcast.375), kind=kOutput, calls=%fused_computation.35 | convolution fusion | flops 549445632 | bytes 35717120 | tf_op jit(solution)/shard_map/qhd,khd->hqk/dot_general | solution.py:184
  362.8 16.4 %multiply_reduce_fusion = (f32[16,512]{1,0:T(8,128)}, f32[16,512,640]{2,1,0:T(8,128)}) fusion(f32[16,512,640]{2,1,0:T(8,128)} %copy-done.1, f32[16,512]{1,0:T(8,128)S(1)} %copy-done.90, bf16[512,16,64]{0,2,1:T(8,128)(2,1)S(1)} %bitcast.358, bf16[640,16,64]{0,2,1:T(8,128)(2,1)S(1)} %bitcast.371), kind=kOutput, calls=%fused_computation.9 | convolution fusion | flops 686809088 | bytes 44367872 | tf_op jit(solution)/shard_map/qhd,khd->hqk/dot_general | solution.py:184
  392.0 11.8 %multiply_reduce_fusion.3 = (f32[16,512]{1,0:T(8,128)}, f32[16,512,512]{1,2,0:T(8,128)}) fusion(f32[16,512,512]{1,2,0:T(8,128)} %get-tuple-element.206, f32[16,512]{1,0:T(8,128)S(1)} %copy-done.94, bf16[512,16,64]{0,2,1:T(8,128)(2,1)S(1)} %bitcast.350, bf16[512,16,64]{0,2,1:T(8,128)(2,1)S(1)} %bitcast.377), kind=kOutput, calls=%fused_computation.38 | convolution fusion | flops 549445632 | bytes 35717120 | tf_op jit(solution)/shard_map/qhd,khd->hqk/dot_general | solution.py:184
  405.9 15.7 %multiply_reduce_fusion.1 = (f32[16,512]{1,0:T(8,128)}, f32[16,512,640]{2,1,0:T(8,128)}) fusion(f32[16,512,640]{2,1,0:T(8,128)} %copy-done.2, f32[16,512]{1,0:T(8,128)S(1)} %copy-done.91, bf16[512,16,64]{0,2,1:T(8,128)(2,1)} %bitcast.354, bf16[640,16,64]{0,2,1:T(8,128)(2,1)} %bitcast.373), kind=kOutput, calls=%fused_computation.12 | convolution fusion | flops 686809088 | bytes 44367872 | tf_op jit(solution)/shard_map/qhd,khd->hqk/dot_general | solution.py:184
  454.8 16.9 %fusion.93 = bf16[1,1024,1024]{1,2,0:T(8,128)(2,1)} fusion(f32[1024,1024]{0,1:T(8,128)} %copy-done.45, f32[1024]{0:T(1024)S(1)} %convert_element_type.228, bf16[4096,1024]{1,0:T(8,128)(2,1)} %param.51, f32[1024,4096]{1,0:T(8,128)} %fusion.92, f32[4096]{0:T(1024)S(1)} %copy-done.138), kind=kOutput, calls=%fused_computation.149 | convolution fusion | flops 8635023360 | bytes 31477760 | tf_op jit(solution)/shard_map/dot_general | solution.py:161
  471.7 17.5 %fusion.91 = bf16[1,1024,1024]{1,2,0:T(8,128)(2,1)} fusion(f32[1024,1024]{0,1:T(8,128)} %copy-done.47, f32[1024]{0:T(1024)S(1)} %convert_element_type.228, bf16[4096,1024]{1,0:T(8,128)(2,1)} %param.51, f32[1024,4096]{1,0:T(8,128)} %fusion.90, f32[4096]{0:T(1024)S(1)} %copy-done.138), kind=kOutput, calls=%fused_computation.147 | convolution fusion | flops 8635023360 | bytes 31477760 | tf_op jit(solution)/shard_map/dot_general | solution.py:161
  496.7 11.8 %multiply_convert_fusion.2 = bf16[16,512,512]{1,2,0:T(8,128)(2,1)S(1)} fusion(f32[16,512,512]{1,2,0:T(8,128)} %get-tuple-element.221, f32[16,512,512]{1,2,0:T(8,128)} %get-tuple-element.196, f32[16,512]{1,0:T(8,128)S(1)} %copy-done.107, f32[16,512]{1,0:T(8,128)S(1)} %copy-done.93), kind=kLoop, calls=%fused_computation.34 | loop fusion | flops 16777216 | bytes 42008576 | tf_op jit(solution)/shard_map/convert_element_type | solution.py:193
  515.5 9.8 %fusion.143 = f32[512,16,64]{0,2,1:T(8,128)} fusion(bf16[512,16,64]{0,2,1:T(8,128)(2,1)S(1)} %bitcast.353, f32[16,512,512]{1,2,0:T(8,128)} %get-tuple-element.206, f32[16,512]{1,0:T(8,128)S(1)} %copy-done.94), kind=kOutput, calls=%fused_computation.197 | convolution fusion | flops 545259520 | bytes 19955712 | tf_op jit(solution)/shard_map/hqk,qhd->khd/dot_general | solution.py:218
  525.3 11.9 %multiply_convert_fusion.3 = bf16[16,512,512]{1,2,0:T(8,128)(2,1)S(1)} fusion(f32[16,512,512]{1,2,0:T(8,128)} %get-tuple-element.213, f32[16,512,512]{1,2,0:T(8,128)} %get-tuple-element.206, f32[16,512]{1,0:T(8,128)S(1)} %copy-done.103, f32[16,512]{1,0:T(8,128)S(1)} %copy-done.94), kind=kLoop, calls=%fused_computation.37 | loop fusion | flops 16777216 | bytes 42008576 | tf_op jit(solution)/shard_map/convert_element_type | solution.py:193
  546.7 11.4 %fusion.80 = f32[1024,16,64]{0,2,1:T(8,128)} fusion(f32[1024,16,64]{0,2,1:T(8,128)} %scatter-add.36, bf16[512,16,64]{0,2,1:T(8,128)(2,1)S(1)} %bitcast.361, f32[16,512,640]{2,1,0:T(8,128)} %copy-done.1, f32[16,512]{1,0:T(8,128)S(1)} %copy-done.90), kind=kOutput, calls=%fused_computation.134 | convolution fusion | flops 682229760 | bytes 27295744 | tf_op jit(solution)/shard_map/hqk,qhd->khd/dot_general | solution.py:218
  565.9 14.0 %multiply_convert_fusion = bf16[16,512,640]{2,1,0:T(8,128)(2,1)} fusion(f32[16,512,640]{2,1,0:T(8,128)} %get-tuple-element.225, f32[16,512,640]{2,1,0:T(8,128)S(1)} %bitcast.327, f32[16,512]{1,0:T(8,128)S(1)} %copy-done.105, f32[16,512]{1,0:T(8,128)S(1)} %copy-done.90), kind=kLoop, calls=%fused_computation.8 | loop fusion | flops 20971520 | bytes 52494336 | tf_op jit(solution)/shard_map/convert_element_type | solution.py:193
  601.2 11.4 %fusion.82 = f32[1024,16,64]{0,2,1:T(8,128)} fusion(f32[1024,16,64]{0,2,1:T(8,128)} %scatter-add.30, bf16[512,16,64]{0,2,1:T(8,128)(2,1)S(1)} %bitcast.357, f32[16,512,640]{2,1,0:T(8,128)} %copy-done.2, f32[16,512]{1,0:T(8,128)S(1)} %copy-done.92), kind=kOutput, calls=%fused_computation.138 | convolution fusion | flops 682229760 | bytes 27295744 | tf_op jit(solution)/shard_map/hqk,qhd->khd/dot_general | solution.py:218
  620.4 14.4 %multiply_convert_fusion.1 = bf16[16,512,640]{2,1,0:T(8,128)(2,1)} fusion(f32[16,512,640]{2,1,0:T(8,128)} %get-tuple-element.217, f32[16,512,640]{2,1,0:T(8,128)S(1)} %bitcast.329, f32[16,512]{1,0:T(8,128)S(1)} %copy-done.101, f32[16,512]{1,0:T(8,128)S(1)} %copy-done.92), kind=kLoop, calls=%fused_computation.11 | loop fusion | flops 20971520 | bytes 52494336 | tf_op jit(solution)/shard_map/convert_element_type | solution.py:193
  663.0 11.0 %fusion.70 = (f32[1024]{0:T(1024)S(1)}, f32[1024]{0:T(1024)S(1)}, f32[1024,1024]{0,1:T(8,128)S(1)}) fusion(bf16[1,1,1024,1024]{2,3,1,0:T(8,128)(2,1)S(1)} %copy-done.10, f32[1024]{0:T(1024)S(1)} %copy-done.121, f32[1024]{0:T(1024)S(1)} %copy-done.116, f32[1024,1024]{0,1:T(8,128)S(1)} %fusion.48, f32[1024]{0:T(1024)S(1)} %copy-done.114, ...), kind=kOutput, calls=%fused_computation.108 | convolution fusion | flops 6471809024 | bytes 25186304 | tf_op jit(solution)/shard_map/dot_general | solution.py:31
  706.8 38.4 %psum.8 = bf16[1,10,2048]{2,1,0:T(8,128)(2,1)S(1)} all-reduce(bf16[1,10,2048]{2,1,0:T(8,128)(2,1)} %reduce-scatter.2.cloned.1.call-done), channel_id=1, replica_groups=mesh['batch'=8,'task'=4] {'batch'}, use_global_device_ids=true, to_apply=%region_42.43 | all-reduce | flops 20480 | bytes 81920 | tf_op jit(solution)/shard_map/psum | solution.py:311
  (541 shorter events, 372.6 us)
Async XLA Ops:
  7.2 144.1 %copy-start = (bf16[1024,1024]{1,0:T(8,128)(2,1)S(1)}, bf16[1024,1024]{1,0:T(8,128)(2,1)}, u32[]{:S(2)}) copy-start(bf16[1024,1024]{1,0:T(8,128)(2,1)} %param.45) | copy-start | bytes 6291460
  7.2 699.6 %reduce-scatter.2.cloned.1.call-start = ((), (), s32[]{:S(2)}) async-start(), calls=%async_computation.1 | async-start | bytes 327680 | tf_op jit(solution)/shard_map/reduce_scatter | solution.py:312
  58.0 28.7 %copy-start.157 = (s32[2,1,16]{2,1,0:T(1,128)S(1)}, s32[2,1,16]{2,1,0:T(1,128)}, u32[]{:S(2)}) copy-start(s32[2,1,16]{2,1,0:T(1,128)} %param.40) | copy-start | bytes 388
  58.0 28.9 %copy-start.144 = (s32[1,1,512]{2,1,0:T(1,128)S(1)}, s32[1,1,512]{2,1,0:T(1,128)}, u32[]{:S(2)}) copy-start(s32[1,1,512]{2,1,0:T(1,128)} %get-tuple-element.175) | copy-start | bytes 6148
  58.0 28.9 %copy-start.145 = (s32[1,1,512]{2,1,0:T(1,128)S(1)}, s32[1,1,512]{2,1,0:T(1,128)}, u32[]{:S(2)}) copy-start(s32[1,1,512]{2,1,0:T(1,128)} %get-tuple-element.176) | copy-start | bytes 6148
  59.5 34.6 %copy-start.11 = (bf16[512,1024]{0,1:T(8,128)(2,1)}, bf16[512,1024]{0,1:T(8,128)(2,1)S(1)}, u32[]{:S(2)}) copy-start(bf16[512,1024]{0,1:T(8,128)(2,1)S(1)} %copy.215) | copy-start | bytes 3145732
  64.5 21.2 %copy-start.97 = (f32[10,512]{1,0:T(8,128)}, f32[10,512]{1,0:T(8,128)S(1)}, u32[]{:S(2)}) copy-start(f32[10,512]{1,0:T(8,128)S(1)} %fusion.174) | copy-start | bytes 61444
  102.7 47.7 %copy-start.82 = (bf16[40,16,64]{2,1,0:T(8,128)(2,1)}, bf16[40,16,64]{2,1,0:T(8,128)(2,1)S(1)}, u32[]{:S(2)}) copy-start(bf16[40,16,64]{2,1,0:T(8,128)(2,1)S(1)} %reshape.848) | copy-start | bytes 245764
  113.3 37.1 %copy-start.20 = (f32[16,512,40]{1,2,0:T(8,128)}, f32[16,512,40]{1,2,0:T(8,128)S(1)}, u32[]{:S(2)}) copy-start(f32[16,512,40]{1,2,0:T(8,128)S(1)} %get-tuple-element.198) | copy-start | bytes 3932164
  201.4 25.9 %copy-start.27 = (f32[16,512,40]{1,2,0:T(8,128)}, f32[16,512,40]{1,2,0:T(8,128)S(1)}, u32[]{:S(2)}) copy-start(f32[16,512,40]{1,2,0:T(8,128)S(1)} %get-tuple-element.208) | copy-start | bytes 3932164
  296.1 35.7 %copy-start.131 = (f32[1024]{0:T(1024)S(1)}, f32[1024]{0:T(1024)}, u32[]{:S(2)}) copy-start(f32[1024]{0:T(1024)} %copy-done.130) | copy-start | bytes 12292
  296.2 35.7 %copy-start.129 = (f32[1024]{0:T(1024)S(1)}, f32[1024]{0:T(1024)}, u32[]{:S(2)}) copy-start(f32[1024]{0:T(1024)} %copy-done.128) | copy-start | bytes 12292
  347.3 31.9 %copy-start.40 = (bf16[512,1024]{0,1:T(8,128)(2,1)}, bf16[512,1024]{0,1:T(8,128)(2,1)S(1)}, u32[]{:S(2)}) copy-start(bf16[512,1024]{0,1:T(8,128)(2,1)S(1)} %get-tuple-element.167) | copy-start | bytes 3145732
  546.7 19.2 %slice-start = ((s8[20971520]{0:T(1024)(128)(4,1)}), s8[4194304]{0:T(1024)(128)(4,1)S(1)}, s32[]{:S(2)}) async-start(s8[20971520]{0:T(1024)(128)(4,1)} %bitcast.326), calls=%async_computation.2 | async-start | bytes 8388608
  546.7 19.2 %slice-start.1 = ((s8[20971520]{0:T(1024)(128)(4,1)}), s8[4194304]{0:T(1024)(128)(4,1)S(1)}, s32[]{:S(2)}) async-start(s8[20971520]{0:T(1024)(128)(4,1)} %bitcast.326), calls=%async_computation.3 | async-start | bytes 8388608
  546.7 19.2 %slice-start.2 = ((s8[20971520]{0:T(1024)(128)(4,1)}), s8[4194304]{0:T(1024)(128)(4,1)S(1)}, s32[]{:S(2)}) async-start(s8[20971520]{0:T(1024)(128)(4,1)} %bitcast.326), calls=%async_computation.4 | async-start | bytes 8388608
  546.7 19.2 %slice-start.3 = ((s8[20971520]{0:T(1024)(128)(4,1)}), s8[4194304]{0:T(1024)(128)(4,1)S(1)}, s32[]{:S(2)}) async-start(s8[20971520]{0:T(1024)(128)(4,1)} %bitcast.326), calls=%async_computation.5 | async-start | bytes 8388608
  601.2 19.2 %slice-start.5 = ((s8[20971520]{0:T(1024)(128)(4,1)}), s8[4194304]{0:T(1024)(128)(4,1)S(1)}, s32[]{:S(2)}) async-start(s8[20971520]{0:T(1024)(128)(4,1)} %bitcast.328), calls=%async_computation.7 | async-start | bytes 8388608
  601.2 19.2 %slice-start.6 = ((s8[20971520]{0:T(1024)(128)(4,1)}), s8[4194304]{0:T(1024)(128)(4,1)S(1)}, s32[]{:S(2)}) async-start(s8[20971520]{0:T(1024)(128)(4,1)} %bitcast.328), calls=%async_computation.8 | async-start | bytes 8388608
  601.2 19.2 %slice-start.7 = ((s8[20971520]{0:T(1024)(128)(4,1)}), s8[4194304]{0:T(1024)(128)(4,1)S(1)}, s32[]{:S(2)}) async-start(s8[20971520]{0:T(1024)(128)(4,1)} %bitcast.328), calls=%async_computation.9 | async-start | bytes 8388608
  601.2 19.2 %slice-start.8 = ((s8[20971520]{0:T(1024)(128)(4,1)}), s8[4194304]{0:T(1024)(128)(4,1)S(1)}, s32[]{:S(2)}) async-start(s8[20971520]{0:T(1024)(128)(4,1)} %bitcast.328), calls=%async_computation.10 | async-start | bytes 8388608
  700.5 44.7 %copy-start.98 = (f32[10,512]{1,0:T(8,128)S(1)}, f32[10,512]{1,0:T(8,128)}, u32[]{:S(2)}) copy-start(f32[10,512]{1,0:T(8,128)} %copy-done.97) | copy-start | bytes 61444
  700.5 47.6 %copy-start.79 = (bf16[1,1024,512]{2,1,0:T(8,128)(2,1)S(1)}, bf16[1,1024,512]{2,1,0:T(8,128)(2,1)}, u32[]{:S(2)}) copy-start(bf16[1,1024,512]{2,1,0:T(8,128)(2,1)} %param.54) | copy-start | bytes 3145732
  700.5 47.9 %copy-start.109 = (bf16[1,10,1024]{2,1,0:T(8,128)(2,1)S(1)}, bf16[1,10,1024]{2,1,0:T(8,128)(2,1)}, u32[]{:S(2)}) copy-start(bf16[1,10,1024]{2,1,0:T(8,128)(2,1)} %param.53) | copy-start | bytes 61444
  (151 other events, 956.9 us)
Sparse Core Ops, SparseCore 0:
  454.2 21.3 reduce-scatter.1
where the time goes:
time: 770 us; the launch traced here: 764 us
  matrix products  417 us (54%)
  other arithmetic  158 us (21%)
  local copies, waits for them, and re-layouts  115 us (15%)
  blocking collectives  57 us (7%)
  between operations  16.2 us (2%)
    dot_general x6, matrix products, contract_last(): lax.dot_general(left, right, (((1,), (1,)), ((), ())), preferred_element_...  93.3 us
    dot_general x4, matrix products, row_pass(): jnp.einsum('qhd,khd->hqk', grad_block, value_window, preferred_element_ty...  55.8 us
    convert_element_type x4, other arithmetic, row_pass(): own_grad = (own_probs * (own_dprobs - delta)).astype(jnp.bfloat16)  52.1 us
    unnamed x356, local copies, waits for them, and re-layouts  51.6 us
    dot_general x4, matrix products, row_pass(): jnp.einsum('hqk,qhd->khd', own_probs.astype(jnp.bfloat16), grad_block, pr...  40.2 us
    psum x1, blocking collectives, on_device(): everything = lax.psum(grad_states.astype(jnp.bfloat16), 'batch')  38.4 us
    dot_general x4, matrix products, row_pass(): jnp.einsum('hqk,khd->qhd', own_probs, values_all[key_start:start + QB], p...  34.5 us
    dot_general x2, matrix products, row_pass(): jnp.dot(activation, w_proj, preferred_element_type=jnp.float32)  34.4 us
  transfers between devices with their start and end apart: 1, of which 0 were waited for; matrix products, arithmetic and copies ran while one was open for 33% of the time, Pallas kernels for 0%

commit v1 on v0

v1 whole, which is shorter than its diff:
```python
import functools

import jax
import jax.numpy as jnp
from jax import lax
from jax.experimental import pallas as pl
from jax.experimental.pallas import tpu as pltpu
from jax.sharding import PartitionSpec as P

bf16 = jnp.bfloat16
f32 = jnp.float32

HEADS = 16
HEAD_DIM = 64
GROUP = 4
LANES = GROUP * HEAD_DIM
QB = 64
MOST = 128
WIN = MOST + QB
PAD = 16
EPSILON = 1e-05
NEGATIVE = -1e30
LOG2E = 1.4426950408889634
LN2 = 0.6931471805599453
GELU_A = 0.7978845608028654
GELU_B = 0.044715
MIB = 1 << 20
MESH = pl.DeviceIdType.MESH


def dot_nn(left, right):
    return jnp.dot(left, right, preferred_element_type=f32)


def dot_nt(left, right):
    return lax.dot_general(
        left, right, (((1,), (1,)), ((), ())), preferred_element_type=f32
    )


def dot_tn(left, right):
    return lax.dot_general(
        left, right, (((0,), (0,)), ((), ())), preferred_element_type=f32
    )


def row_vector(ref, part=slice(None)):
    return ref[part].astype(f32)[None, :]


def normalise(hidden):
    centred = hidden - jnp.mean(hidden, axis=1, keepdims=True)
    spread = jnp.mean(centred * centred, axis=1, keepdims=True)
    inverse = lax.rsqrt(spread + EPSILON)
    return centred * inverse, inverse


def norm_backward(grad, gain, unit, inverse):
    scaled = grad * gain
    mean_one = jnp.mean(scaled, axis=1, keepdims=True)
    mean_two = jnp.mean(scaled * unit, axis=1, keepdims=True)
    return inverse * (scaled - mean_one - unit * mean_two)


def gelu_both(value, grad):
    square = value * value
    half = 0.5 + 0.5 * jnp.tanh(value * (GELU_A + (GELU_A * GELU_B) * square))
    act = value * half
    slope = half + (act * (2 * GELU_A + (6 * GELU_A * GELU_B) * square)) * (1.0 - half)
    return act.astype(bf16), (grad * slope).astype(bf16)


def barrier_with(peers):
    barrier = pltpu.get_barrier_semaphore()
    for peer in peers:
        pl.semaphore_signal(barrier, inc=1, device_id=peer, device_id_type=MESH)
    return barrier


def qkv_kernel(
    tasks,
    tok_ref,
    gain_ref,
    shift_ref,
    w_ref,
    b_ref,
    embed_ref,
    win_hbm,
    bin_ref,
    wout_hbm,
    bout_ref,
    mixed_ref,
    hidden_ref,
    states_ref,
    win,
    wout,
    padded,
    own,
    gathered,
    load_sem,
    send_sem,
    recv_sem,
):
    step = pl.program_id(0)
    steps = pl.num_programs(0)
    row_axis = lax.axis_index("batch")
    me = lax.axis_index("task")
    peers = [(row_axis, lax.rem(me + k, tasks)) for k in range(1, tasks)]

    def load(index):
        source, target = ((win_hbm, win), (wout_hbm, wout))[index]
        return pltpu.make_async_copy(source.at[0], target, load_sem.at[index])

    def send(k):
        return pltpu.make_async_remote_copy(
            src_ref=own,
            dst_ref=gathered.at[me],
            send_sem=send_sem.at[k - 1],
            recv_sem=recv_sem.at[k - 1],
            device_id=peers[k - 1],
            device_id_type=MESH,
        )

    @pl.when(step == 0)
    def _():
        load(0).start()
        load(1).start()
        barrier_with(peers)

    @pl.when(step == 1)
    def _():
        load(0).wait()
        load(1).wait()
        padded[...] = jnp.zeros(padded.shape, f32)
        padded[: embed_ref.shape[1], :] = embed_ref[0].astype(f32)
        pre = dot_nn(padded[...].astype(bf16), win[...]) + bin_ref[...].astype(f32)
        hidden = jnp.tanh(pre)
        hidden_ref[...] = hidden
        states = dot_nn(hidden.astype(bf16), wout[...]) + bout_ref[...].astype(f32)
        states = states.astype(bf16)
        own[...] = states
        gathered[me] = states
        pl.semaphore_wait(pltpu.get_barrier_semaphore(), tasks - 1)
        for k in range(1, tasks):
            send(k).start()

    normed, _ = normalise(tok_ref[...].astype(f32))
    normed = (normed * row_vector(gain_ref) + row_vector(shift_ref)).astype(bf16)
    width = tok_ref.shape[1]
    mixed = dot_nn(normed, w_ref[...]) + row_vector(b_ref)
    mixed_ref[:, :width] = (mixed[:, :width] * (HEAD_DIM ** (-0.5) * LOG2E)).astype(bf16)
    mixed_ref[:, width:] = mixed[:, width:].astype(bf16)

    @pl.when(step == steps - 1)
    def _():
        for k in range(1, tasks):
            send(k).wait()
        states_ref[...] = gathered[...].reshape(states_ref.shape)


def qkv_call(tasks, tokens, gain, shift, w_qkv, b_qkv, embed, w_in, b_in, w_out, b_out):
    micro, rows, seq, width = tokens.shape
    tile = 512
    per_row = seq // tile
    rank = w_in.shape[2]
    whole1 = lambda x: pl.BlockSpec(x.shape, lambda i: (0,) * x.ndim)
    once = lambda x: pl.BlockSpec(
        x.shape, lambda i: (0,) * x.ndim, pipeline_mode=pl.Buffered(1)
    )
    return pl.pallas_call(
        functools.partial(qkv_kernel, tasks),
        grid=(micro * rows * per_row,),
        in_specs=[
            pl.BlockSpec(
                (None, None, tile, width),
                lambda i: (i // (rows * per_row), (i // per_row) % rows, i % per_row, 0),
            ),
            whole1(gain),
            whole1(shift),
            once(w_qkv),
            whole1(b_qkv),
            whole1(embed),
            pl.BlockSpec(memory_space=pl.ANY),
            whole1(b_in),
            pl.BlockSpec(memory_space=pl.ANY),
            whole1(b_out),
        ],
        out_specs=[
            pl.BlockSpec((tile, 3 * width), lambda i: (i, 0)),
            pl.BlockSpec((PAD, rank), lambda i: (0, 0)),
            pl.BlockSpec((tasks * PAD, 2 * width), lambda i: (0, 0)),
        ],
        out_shape=[
            jax.ShapeDtypeStruct((micro * rows * seq, 3 * width), bf16),
            jax.ShapeDtypeStruct((PAD, rank), f32),
            jax.ShapeDtypeStruct((tasks * PAD, 2 * width), bf16),
        ],
        scratch_shapes=[
            pltpu.VMEM(w_in.shape[1:], bf16),
            pltpu.VMEM(w_out.shape[1:], bf16),
            pltpu.VMEM((PAD, width), f32),
            pltpu.VMEM((PAD, 2 * width), bf16),
            pltpu.VMEM((tasks, PAD, 2 * width), bf16),
            pltpu.SemaphoreType.DMA((2,)),
            pltpu.SemaphoreType.DMA((tasks - 1,)),
            pltpu.SemaphoreType.DMA((tasks - 1,)),
        ],
        compiler_params=pltpu.CompilerParams(
            collective_id=0, has_side_effects=True, vmem_limit_bytes=40 * MIB
        ),
        name="norm_qkv",
    )(tokens, gain, shift, w_qkv, b_qkv, embed, w_in, b_in, w_out, b_out)


def stack_heads(block):
    lane = lax.broadcasted_iota(jnp.int32, (QB, 128), 1)
    zero = jnp.zeros((QB, 128), block.dtype)
    rows = []
    for h in range(GROUP):
        part = jnp.where((lane < HEAD_DIM) == (h % 2 == 0), block[:, (h // 2) * 128 :][:, :128], zero)
        rows.append(jnp.concatenate([part, zero] if h < 2 else [zero, part], axis=1))
    return jnp.concatenate(rows, axis=0)


def pick_heads(stacked):
    lane = lax.broadcasted_iota(jnp.int32, (QB, 128), 1)
    low = jnp.where(lane < HEAD_DIM, stacked[:QB, :128], stacked[QB : 2 * QB, :128])
    high = jnp.where(lane < HEAD_DIM, stacked[2 * QB : 3 * QB, 128:], stacked[3 * QB :, 128:])
    return jnp.concatenate([low, high], axis=1)


def fill_mask(seg_ref, task_ref, micro, prefix, bias, by_key):
    segments = seg_ref[...]
    seq = segments.shape[1]
    token_task = jnp.zeros(segments.shape, jnp.int32)
    for s in range(task_ref.shape[-1]):
        token_task = jnp.where(segments == s, task_ref[micro, 0, s], token_task)
    segments = segments.astype(f32)
    for c in range(0, seq, 128):
        by_key[c : c + 128, :] = jnp.broadcast_to(segments[:, c : c + 128], (128, 128)).T
    for b in range(seq // QB):
        start = max(b * QB - MOST, 0)

        def twice(x):
            part = x[:, b * QB : (b + 1) * QB]
            return jnp.concatenate([part, part], axis=1)

        key_pos = start + lax.broadcasted_iota(jnp.int32, (WIN, 128), 0)
        query_pos = b * QB + (lax.broadcasted_iota(jnp.int32, (WIN, 128), 1) & (QB - 1))
        own = (by_key[start : start + WIN, :] == twice(segments)) & (key_pos <= query_pos)
        bias[b, :WIN, :] = jnp.where(own, 0.0, NEGATIVE)
        index = lax.broadcasted_iota(jnp.int32, (bias.shape[1] - WIN, 128), 0)
        fits = (lax.shift_right_logical(index, 4) == twice(token_task)) & (
            (index & (PAD - 1)) < prefix
        )
        bias[b, WIN:, :] = jnp.where(fits, 0.0, NEGATIVE)


def attention_kernel(
    prefix, task_ref, seg_ref, q_ref, k_ref, v_ref, pk_ref, pv_ref, out_ref, probs_ref, bias, by_key
):
    micro = pl.program_id(0)

    @pl.when(pl.program_id(1) == 0)
    def _():
        fill_mask(seg_ref, task_ref, micro, prefix, bias, by_key)

    for b in range(q_ref.shape[0] // QB):
        rows = slice(b * QB, (b + 1) * QB)
        start = max(b * QB - MOST, 0)
        window = slice(start, start + WIN)
        keys = jnp.concatenate([k_ref[window, :], pk_ref[...]], axis=0)
        values = jnp.concatenate([v_ref[window, :], pv_ref[...]], axis=0)
        scores = dot_nt(keys, stack_heads(q_ref[rows, :]))
        scores = scores + jnp.concatenate([bias[b], bias[b]], axis=1)
        powers = jnp.exp2(scores - jnp.max(scores, axis=0, keepdims=True))
        total = jnp.sum(powers, axis=0, keepdims=True)
        probs = (powers * (1.0 / total)).astype(bf16)
        probs_ref[b] = probs
        out_ref[rows, :] = pick_heads(dot_tn(probs, values)).astype(bf16)


def attention_call(mixed, segments, tasks, states, prefix):
    micro, _, seq = segments.shape
    width = mixed.shape[1] // 3
    groups = width // LANES
    blocks = seq // QB
    keys = WIN + states.shape[0]
    part = lambda offset: pl.BlockSpec((seq, LANES), lambda r, g: (r, offset + g))
    piece = lambda offset: pl.BlockSpec((states.shape[0], LANES), lambda r, g: (0, offset + g))
    return pl.pallas_call(
        functools.partial(attention_kernel, prefix),
        grid=(micro, groups),
        in_specs=[
            pl.BlockSpec(memory_space=pltpu.SMEM),
            pl.BlockSpec((None, 1, seq), lambda r, g: (r, 0, 0)),
            part(0),
            part(groups),
            part(2 * groups),
            piece(0),
            piece(groups),
        ],
        out_specs=[
            part(0),
            pl.BlockSpec((None, None, blocks, keys, LANES), lambda r, g: (r, g, 0, 0, 0)),
        ],
        out_shape=[
            jax.ShapeDtypeStruct((micro * seq, width), bf16),
            jax.ShapeDtypeStruct((micro, groups, blocks, keys, LANES), bf16),
        ],
        scratch_shapes=[pltpu.VMEM((blocks, keys, 128), f32), pltpu.VMEM((seq, 128), f32)],
        compiler_params=pltpu.CompilerParams(vmem_limit_bytes=24 * MIB),
        name="attention",
    )(tasks, segments, mixed, mixed, mixed, states, states)


def mlp_kernel(
    att_ref,
    tok_ref,
    cot_ref,
    wa_ref,
    ba_ref,
    gain_ref,
    shift_ref,
    wf_ref,
    bf_ref,
    wp_ref,
    bp_ref,
    out_ref,
    gres_ref,
    gatt_ref,
    act_all,
    gpre_all,
):
    w_attn = wa_ref[...]
    gain = row_vector(gain_ref)
    resid = tok_ref[...].astype(f32) + dot_nn(att_ref[...], w_attn) + row_vector(ba_ref)
    unit, inverse = normalise(resid)
    normed = (unit * gain + row_vector(shift_ref)).astype(bf16)
    grad_out = cot_ref[...]
    chunk = 512
    for start in range(0, wf_ref.shape[1], chunk):
        part = slice(start, start + chunk)
        pre = dot_nn(normed, wf_ref[:, part]) + row_vector(bf_ref, part)
        act, gpre = gelu_both(pre, dot_nt(grad_out, wp_ref[part, :]))
        act_all[:, part] = act
        gpre_all[:, part] = gpre
    out = resid + dot_nn(act_all[...], wp_ref[...]) + row_vector(bp_ref)
    out_ref[...] = out.astype(bf16)
    grad_normed = dot_nt(gpre_all[...], wf_ref[...])
    grad_resid = grad_out.astype(f32) + norm_backward(grad_normed, gain, unit, inverse)
    gres_ref[...] = grad_resid
    gatt_ref[...] = dot_nt(grad_resid.astype(bf16), w_attn).astype(bf16)


def mlp_call(attended, tokens, cotangent, w_attn, b_attn, gain, shift, w_fc, b_fc, w_proj, b_proj):
    micro, rows, seq, width = tokens.shape
    tile = 512
    per_row = seq // tile
    flat = pl.BlockSpec((tile, width), lambda i: (i, 0))
    deep = pl.BlockSpec(
        (None, None, tile, width),
        lambda i: (i // (rows * per_row), (i // per_row) % rows, i % per_row, 0),
    )
    once = lambda x: pl.BlockSpec(
        x.shape, lambda i: (0,) * x.ndim, pipeline_mode=pl.Buffered(1)
    )
    weights = (w_attn, b_attn, gain, shift, w_fc, b_fc, w_proj, b_proj)
    count = micro * rows * seq
    return pl.pallas_call(
        mlp_kernel,
        grid=(count // tile,),
        in_specs=[flat, deep, deep] + [once(x) for x in weights],
        out_specs=[deep, flat, flat],
        out_shape=[
            jax.ShapeDtypeStruct(tokens.shape, bf16),
            jax.ShapeDtypeStruct((count, width), f32),
            jax.ShapeDtypeStruct((count, width), bf16),
        ],
        scratch_shapes=[pltpu.VMEM((tile, w_fc.shape[1]), bf16)] * 2,
        compiler_params=pltpu.CompilerParams(vmem_limit_bytes=60 * MIB),
        name="feed_forward",
    )(attended, tokens, cotangent, *weights)


def attention_grad_kernel(
    q_ref,
    k_ref,
    v_ref,
    pk_ref,
    pv_ref,
    probs_ref,
    g_ref,
    dq_ref,
    dk_ref,
    dv_ref,
    dpk_ref,
    dpv_ref,
    key_sum,
    value_sum,
    prefix_key_sum,
    prefix_value_sum,
):
    for b in range(q_ref.shape[0] // QB):
        rows = slice(b * QB, (b + 1) * QB)
        start = max(b * QB - MOST, 0)
        window = slice(start, start + WIN)
        keys = jnp.concatenate([k_ref[window, :], pk_ref[...]], axis=0)
        values = jnp.concatenate([v_ref[window, :], pv_ref[...]], axis=0)
        queries = stack_heads(q_ref[rows, :])
        grads = stack_heads(g_ref[rows, :])
        probs = probs_ref[b]
        weight = probs.astype(f32)
        product = weight * dot_nt(values, grads)
        delta = jnp.sum(product, axis=0, keepdims=True)
        score_grad = (product - weight * delta).astype(bf16)
        dv = dot_nn(probs, grads)
        dk = dot_nn(score_grad, queries)
        dq = pick_heads(dot_tn(score_grad, keys))
        dq_ref[rows, :] = (dq * HEAD_DIM ** (-0.5)).astype(bf16)
        old = 0 if b == 0 else min(WIN, b * QB - start) if start else WIN
        for total, fresh in ((key_sum, dk), (value_sum, dv)):
            if old:
                total[start : start + old, :] += fresh[:old]
            if old < WIN:
                total[start + old : start + WIN, :] = fresh[old:WIN]
        if b == 0:
            prefix_key_sum[...] = dk[WIN:]
            prefix_value_sum[...] = dv[WIN:]
        else:
            prefix_key_sum[...] += dk[WIN:]
            prefix_value_sum[...] += dv[WIN:]
    dk_ref[...] = (key_sum[...] * LN2).astype(bf16)
    dv_ref[...] = value_sum[...].astype(bf16)

    @pl.when(pl.program_id(1) == 0)
    def _():
        dpk_ref[...] = prefix_key_sum[...] * LN2
        dpv_ref[...] = prefix_value_sum[...]

    @pl.when(pl.program_id(1) != 0)
    def _():
        dpk_ref[...] += prefix_key_sum[...] * LN2
        dpv_ref[...] += prefix_value_sum[...]


def attention_grad_call(mixed, states, probs, grad_attended):
    micro, groups, blocks, keys, _ = probs.shape
    seq = blocks * QB
    width = grad_attended.shape[1]
    prefix_rows = states.shape[0]
    part = lambda offset: pl.BlockSpec((seq, LANES), lambda g, r: (r, offset + g))
    piece = lambda offset: pl.BlockSpec((prefix_rows, LANES), lambda g, r: (0, offset + g))
    return pl.pallas_call(
        attention_grad_kernel,
        grid=(groups, micro),
        in_specs=[
            part(0),
            part(groups),
            part(2 * groups),
            piece(0),
            piece(groups),
            pl.BlockSpec((None, None, blocks, keys, LANES), lambda g, r: (r, g, 0, 0, 0)),
            part(0),
        ],
        out_specs=[part(0)] * 3 + [piece(0)] * 2,
        out_shape=[jax.ShapeDtypeStruct((micro * seq, width), bf16)] * 3
        + [jax.ShapeDtypeStruct((prefix_rows, width), f32)] * 2,
        scratch_shapes=[pltpu.VMEM((seq, LANES), f32)] * 2
        + [pltpu.VMEM((prefix_rows, LANES), f32)] * 2,
        compiler_params=pltpu.CompilerParams(vmem_limit_bytes=24 * MIB),
        name="attention_grad",
    )(mixed, mixed, mixed, states, states, probs, grad_attended)


def input_grad_tile(dq_ref, dk_ref, dv_ref, tok_ref, gres_ref, gain_ref, w_ref):
    width = dq_ref.shape[1]
    grad = dot_nt(dq_ref[...], w_ref[:, :width])
    grad = grad + dot_nt(dk_ref[...], w_ref[:, width : 2 * width])
    grad = grad + dot_nt(dv_ref[...], w_ref[:, 2 * width :])
    unit, inverse = normalise(tok_ref[...].astype(f32))
    back = norm_backward(grad, row_vector(gain_ref), unit, inverse)
    return (gres_ref[...] + back).astype(bf16)


def sum_kernel(
    tasks,
    shards,
    dq_ref,
    dk_ref,
    dv_ref,
    tok_ref,
    gres_ref,
    gain_ref,
    w_ref,
    dpk_ref,
    dpv_ref,
    grad_ref,
    summed_ref,
    send_a,
    recv_a,
    send_b,
    recv_b,
    gathered,
    sems,
    sems_b,
):
    step = pl.program_id(0)
    shard = lax.axis_index("batch")
    task = lax.axis_index("task")
    task_peers = [(shard, lax.rem(task + k, tasks)) for k in range(1, tasks)]
    shard_peers = [(lax.rem(shard + k, shards), task) for k in range(1, shards)]
    width = dpk_ref.shape[1]
    lanes = send_b.shape[2]

    def to_task(k):
        return pltpu.make_async_remote_copy(
            src_ref=send_a.at[lax.rem(task + k, tasks)],
            dst_ref=recv_a.at[k - 1],
            send_sem=sems.at[0, k - 1],
            recv_sem=sems.at[1, k - 1],
            device_id=task_peers[k - 1],
            device_id_type=MESH,
        )

    def to_shard(k):
        return pltpu.make_async_remote_copy(
            src_ref=send_b.at[lax.rem(shard + k, shards)],
            dst_ref=recv_b.at[k - 1],
            send_sem=sems_b.at[0, k - 1],
            recv_sem=sems_b.at[1, k - 1],
            device_id=shard_peers[k - 1],
            device_id_type=MESH,
        )

    def back_to_shard(k):
        return pltpu.make_async_remote_copy(
            src_ref=gathered.at[shard],
            dst_ref=gathered.at[shard],
            send_sem=sems_b.at[2, k - 1],
            recv_sem=sems_b.at[3, k - 1],
            device_id=shard_peers[k - 1],
            device_id_type=MESH,
        )

    @pl.when(step == 0)
    def _():
        barrier_with(task_peers + shard_peers)
        for t in range(tasks):
            part = slice(t * PAD, (t + 1) * PAD)
            send_a[t, :, :width] = dpk_ref[part, :].astype(bf16)
            send_a[t, :, width:] = dpv_ref[part, :].astype(bf16)

    @pl.when(step == 1)
    def _():
        pl.semaphore_wait(pltpu.get_barrier_semaphore(), tasks - 1 + shards - 1)
        for k in range(1, tasks):
            to_task(k).start()

    @pl.when(step == 2)
    def _():
        for k in range(1, tasks):
            to_task(k).wait()
        total = send_a[task].astype(f32)
        for k in range(1, tasks):
            total = total + recv_a[k - 1].astype(f32)
        total = total.astype(bf16)
        for c in range(shards):
            send_b[c] = total[:, c * lanes : (c + 1) * lanes]
        for k in range(1, shards):
            to_shard(k).start()

    @pl.when(step == 3)
    def _():
        for k in range(1, shards):
            to_shard(k).wait()
        total = send_b[shard].astype(f32)
        for k in range(1, shards):
            total = total + recv_b[k - 1].astype(f32)
        gathered[shard] = total.astype(bf16)
        for k in range(1, shards):
            back_to_shard(k).start()

    grad_ref[...] = input_grad_tile(
        dq_ref, dk_ref, dv_ref, tok_ref, gres_ref, gain_ref, w_ref
    )

    @pl.when(step == 3)
    def _():
        for k in range(1, shards):
            back_to_shard(k).wait()
        for c in range(shards):
            summed_ref[:, c * lanes : (c + 1) * lanes] = gathered[c]


def sum_call(tasks, shards, dq, dk, dv, tokens, grad_resid, gain, w_qkv, dpk, dpv):
    seq, width = tokens.shape[2:]
    tile = seq // 4
    flat = pl.BlockSpec((tile, width), lambda i: (i, 0))
    once = lambda x: pl.BlockSpec(
        x.shape, lambda i: (0,) * x.ndim, pipeline_mode=pl.Buffered(1)
    )
    lanes = 2 * width // shards
    return pl.pallas_call(
        functools.partial(sum_kernel, tasks, shards),
        grid=(4,),
        in_specs=[flat, flat, flat]
        + [pl.BlockSpec((None, None, tile, width), lambda i: (0, 0, i, 0)), flat]
        + [once(x) for x in (gain, w_qkv, dpk, dpv)],
        out_specs=[flat, pl.BlockSpec((PAD, 2 * width), lambda i: (0, 0))],
        out_shape=[
            jax.ShapeDtypeStruct((seq, width), bf16),
            jax.ShapeDtypeStruct((PAD, 2 * width), bf16),
        ],
        scratch_shapes=[
            pltpu.VMEM((tasks, PAD, 2 * width), bf16),
            pltpu.VMEM((tasks - 1, PAD, 2 * width), bf16),
            pltpu.VMEM((shards, PAD, lanes), bf16),
            pltpu.VMEM((shards - 1, PAD, lanes), bf16),
            pltpu.VMEM((shards, PAD, lanes), bf16),
            pltpu.SemaphoreType.DMA((2, tasks - 1)),
            pltpu.SemaphoreType.DMA((4, shards - 1)),
        ],
        compiler_params=pltpu.CompilerParams(
            collective_id=1, has_side_effects=True, vmem_limit_bytes=32 * MIB
        ),
        name="grad_first_sum",
    )(dq, dk, dv, tokens, grad_resid, gain, w_qkv, dpk, dpv)


def last_kernel(
    dq_ref,
    dk_ref,
    dv_ref,
    tok_ref,
    gres_ref,
    gain_ref,
    w_ref,
    first_hbm,
    summed_ref,
    hidden_ref,
    embed_ref,
    win_ref,
    wout_ref,
    out_hbm,
    gembed_ref,
    gin_hbm,
    gbin_ref,
    gout_hbm,
    gbout_ref,
    tile_out,
    padded,
    gin,
    gout,
    sems,
):
    step = pl.program_id(0)
    steps = pl.num_programs(0)
    tile = dq_ref.shape[0]

    def pass_on():
        return pltpu.make_async_copy(first_hbm, out_hbm.at[0, 0], sems.at[0])

    def put_in():
        return pltpu.make_async_copy(gin, gin_hbm.at[0], sems.at[1])

    def put_out():
        return pltpu.make_async_copy(gout, gout_hbm.at[0], sems.at[2])

    def put_tile(index):
        return pltpu.make_async_copy(
            tile_out.at[index],
            out_hbm.at[out_hbm.shape[0] - 1, 0, pl.ds(index * tile, tile), :],
            sems.at[3 + index],
        )

    @pl.when(step == 0)
    def _():
        pass_on().start()
        summed = summed_ref[...]
        hidden = hidden_ref[...]
        gout[...] = dot_tn(hidden.astype(bf16), summed)
        put_out().start()
        gbout_ref[...] = jnp.sum(summed.astype(f32), axis=0, keepdims=True)
        grad_hidden = dot_nt(summed, wout_ref[0])
        grad_pre = (grad_hidden * (1.0 - hidden * hidden)).astype(bf16)
        padded[...] = jnp.zeros(padded.shape, f32)
        padded[: embed_ref.shape[1], :] = embed_ref[0].astype(f32)
        gin[...] = dot_tn(padded[...].astype(bf16), grad_pre)
        put_in().start()
        gbin_ref[...] = jnp.sum(grad_pre.astype(f32), axis=0, keepdims=True)
        gembed_ref[0] = dot_nt(grad_pre, win_ref[0])[: embed_ref.shape[1], :]

    result = input_grad_tile(dq_ref, dk_ref, dv_ref, tok_ref, gres_ref, gain_ref, w_ref)
    for index in range(tile_out.shape[0]):

        @pl.when(step == index)
        def _():
            tile_out[index] = result
            put_tile(index).start()

    @pl.when(step == steps - 1)
    def _():
        pass_on().wait()
        put_in().wait()
        put_out().wait()
        for index in range(tile_out.shape[0]):
            put_tile(index).wait()


def last_call(dq, dk, dv, tokens, grad_resid, gain, w_qkv, first, summed, hidden, embed, w_in, w_out):
    micro, _, seq, width = tokens.shape
    tile = 512
    tiles = seq // tile
    flat = pl.BlockSpec((tile, width), lambda i: ((micro - 1) * tiles + i, 0))
    anywhere = pl.BlockSpec(memory_space=pl.ANY)
    once = lambda x: pl.BlockSpec(
        x.shape, lambda i: (0,) * x.ndim, pipeline_mode=pl.Buffered(1)
    )
    whole = lambda shape: pl.BlockSpec(shape, lambda i: (0,) * len(shape))
    rank = w_in.shape[2]
    return pl.pallas_call(
        last_kernel,
        grid=(tiles,),
        in_specs=[flat, flat, flat]
        + [pl.BlockSpec((None, None, tile, width), lambda i: (micro - 1, 0, i, 0)), flat]
        + [once(gain), once(w_qkv), anywhere]
        + [once(x) for x in (summed, hidden, embed, w_in, w_out)],
        out_specs=[
            anywhere,
            whole(embed.shape),
            anywhere,
            whole((1, rank)),
            anywhere,
            whole((1, 2 * width)),
        ],
        out_shape=[
            jax.ShapeDtypeStruct(tokens.shape, bf16),
            jax.ShapeDtypeStruct(embed.shape, f32),
            jax.ShapeDtypeStruct(w_in.shape, f32),
            jax.ShapeDtypeStruct((1, rank), f32),
            jax.ShapeDtypeStruct(w_out.shape, f32),
            jax.ShapeDtypeStruct((1, 2 * width), f32),
        ],
        scratch_shapes=[
            pltpu.VMEM((tiles, tile, width), bf16),
            pltpu.VMEM((PAD, width), f32),
            pltpu.VMEM(w_in.shape[1:], f32),
            pltpu.VMEM(w_out.shape[1:], f32),
            pltpu.SemaphoreType.DMA((3 + tiles,)),
        ],
        compiler_params=pltpu.CompilerParams(vmem_limit_bytes=48 * MIB),
        name="grad_last",
    )(dq, dk, dv, tokens, grad_resid, gain, w_qkv, first, summed, hidden, embed, w_in, w_out)


def on_device(
    tasks,
    shards,
    tokens,
    cotangent,
    segment_ids,
    task_ids,
    ln1_gain,
    ln1_bias,
    w_qkv,
    b_qkv,
    w_attn_out,
    b_attn_out,
    ln2_gain,
    ln2_bias,
    w_fc,
    b_fc,
    w_proj,
    b_proj,
    prefix_embed,
    reparam_in,
    reparam_in_bias,
    reparam_out,
    reparam_out_bias,
):
    mixed, hidden, states = qkv_call(
        tasks,
        tokens,
        ln1_gain,
        ln1_bias,
        w_qkv,
        b_qkv,
        prefix_embed,
        reparam_in,
        reparam_in_bias,
        reparam_out,
        reparam_out_bias,
    )
    attended, probs = attention_call(
        mixed, segment_ids, task_ids, states, prefix_embed.shape[1]
    )
    block_out, grad_resid, grad_attended = mlp_call(
        attended,
        tokens,
        cotangent,
        w_attn_out,
        b_attn_out,
        ln2_gain,
        ln2_bias,
        w_fc,
        b_fc,
        w_proj,
        b_proj,
    )
    dq, dk, dv, dpk, dpv = attention_grad_call(mixed, states, probs, grad_attended)
    first, summed = sum_call(
        tasks, shards, dq, dk, dv, tokens, grad_resid, ln1_gain, w_qkv, dpk, dpv
    )
    input_grad, gembed, gin, gbin, gout, gbout = last_call(
        dq,
        dk,
        dv,
        tokens,
        grad_resid,
        ln1_gain,
        w_qkv,
        first,
        summed,
        hidden,
        prefix_embed,
        reparam_in,
        reparam_out,
    )
    return (block_out, input_grad, gembed, gin, gbin, gout, gbout)


def solution(mesh):
    split = ("batch", "task")
    in_specs = (
        (P(None, split, None, None),) * 2
        + (P(None, split, None),) * 2
        + (P(),) * 12
        + (
            P("task", None, None),
            P("task", None, None),
            P("task", None),
            P("task", None, None),
            P("task", None),
        )
    )
    out_specs = (
        P(None, split, None, None),
        P(None, split, None, None),
        P("task", None, None),
        P("task", None, None),
        P("task", None),
        P("task", None, None),
        P("task", None),
    )
    return jax.shard_map(
        functools.partial(on_device, mesh.shape["task"], mesh.shape["batch"]),
        mesh=mesh,
        in_specs=in_specs,
        out_specs=out_specs,
        check_vma=False,
    )
```

time: 770 us -> 274 us (0.36)
  matrix products: 417 us -> 0 us
  Pallas kernels: 0 us -> 236 us
  other arithmetic: 158 us -> 0 us
  local copies, waits for them, and re-layouts: 115 us -> 37.1 us
  blocking collectives: 57 us -> 0 us
  between operations: 16.2 us -> 1.21 us
    dot_general x68 -> x0, matrix products: 417 us -> none  [the longest x6 93.3 us: contract_last(): lax.dot_general(left, right, (((1,), (1,)), ((), ())), preferred_element_...]
    pallas_call x0 -> x6, Pallas kernels: none -> 236 us  [the longest x1 107 us: mlp_call(): pl.pallas_call(mlp_kernel, grid=(count // tile,), in_specs=[flat, deep, d...]
    convert_element_type x17 -> x0, other arithmetic: 63.1 us -> none  [the longest x4 52.1 us: row_pass(): own_grad = (own_probs * (own_dprobs - delta)).astype(jnp.bfloat16)]
    reduce_sum x18 -> x0, other arithmetic: 47.9 us -> none  [the longest x4 26.1 us: row_pass(): jnp.sum(own_exp, axis=2, keepdims=True)]
    slice x26 -> x0, local copies, waits for them, and re-layouts: 42 us -> none  [the longest x8 18.2 us: block_scores(): keys_all[key_start:block_end]]
    psum x1 -> x0, blocking collectives: 38.4 us -> none  [on_device(): everything = lax.psum(grad_states.astype(jnp.bfloat16), 'batch')]
    another operation x5 -> x0, other arithmetic: 26 us -> none
    all_gather x1 -> x0, blocking collectives: 18.6 us -> none  [on_device(): states = lax.all_gather(own_states, 'task', axis=0, tiled=True)]
  transfers between devices with their start and end apart: 1 -> 0, of which waited for: 0 -> 0; matrix products, arithmetic and copies ran while one was open for 33% -> 0% of each run, Pallas kernels for 0% -> 0%
where the time goes in v1:
time: 274 us; the launch traced here: 275 us
  Pallas kernels  236 us (86%)
  local copies, waits for them, and re-layouts  37.1 us (14%)
    pallas_call x1, Pallas kernels, mlp_call(): pl.pallas_call(mlp_kernel, grid=(count // tile,), in_specs=[flat, deep, d...  107 us
    pallas_call x1, Pallas kernels, attention_grad_call(): pl.pallas_call(attention_grad_kernel, grid=(groups, micro), in_specs=[par...  49 us
    unnamed x53, local copies, waits for them, and re-layouts  37.1 us
    pallas_call x1, Pallas kernels, sum_call(): pl.pallas_call(functools.partial(sum_kernel, tasks, shards), grid=(4,), i...  22.4 us
    pallas_call x1, Pallas kernels, attention_call(): pl.pallas_call(functools.partial(attention_kernel, prefix), grid=(micro,...  22.1 us
    pallas_call x1, Pallas kernels, qkv_call(): pl.pallas_call(functools.partial(qkv_kernel, tasks), grid=(micro * rows *...  18.6 us
    pallas_call x1, Pallas kernels, last_call(): pl.pallas_call(last_kernel, grid=(tiles,), in_specs=[flat, flat, flat] +...  17.6 us

profile of v1, /device:TPU:0, one launch (start us, length us, event | category | flops | bytes accessed | tf_op | source)
XLA Modules:
  0.0 274.6 jit_solution(8704226283446207860)
XLA Ops:
  0.6 2.2 copy-done.2
  2.8 2.8 %copy-done.4 = bf16[1024,3072]{1,0:T(8,128)(2,1)S(1)} copy-done((bf16[1024,3072]{1,0:T(8,128)(2,1)S(1)}, bf16[1024,3072]{1,0:T(8,128)(2,1)}, u32[]{:S(2)}) %copy-start.4) | copy-done | bytes 6291480
  5.6 1.6 copy-done.10
  7.2 1.2 copy-done.14
  8.4 0.8 copy-done.16
  9.2 0.7 copy-done.18
  9.9 0.7 copy-done.20
  10.6 0.7 copy-done.22
  11.9 0.7 copy-done.24
  12.6 18.6 %norm_qkv.1 = (bf16[2048,3072]{1,0:T(8,128)(2,1)}, f32[16,512]{1,0:T(8,128)S(1)}, bf16[64,2048]{1,0:T(8,128)(2,1)S(1)}) custom-call(bf16[2,1,1024,1024]{3,2,1,0:T(8,128)(2,1)S(1)} %copy-done.2, bf16[1024]{0:T(1024)(128)(2,1)S(1)} %copy-done.18, bf16[1024]{0:T(1024)(128)(2,1)S(1)} %copy-done.23, bf16[1024,3072]{1,0:T(8,128)(2,1)S(1)} %copy-done.4, ...), custom_call_target="tpu_custom_call" | custom-call | tf_op jit(solution)/shard_map/norm_qkv/pallas_call | solution.py:170
  31.3 4.6 %copy-done = bf16[2048,3072]{1,0:T(8,128)(2,1)S(1)} copy-done((bf16[2048,3072]{1,0:T(8,128)(2,1)S(1)}, bf16[2048,3072]{1,0:T(8,128)(2,1)}, u32[]{:S(2)}) %copy-start) | copy-done | bytes 12582936
  35.8 22.1 %attention.1 = (bf16[2048,1024]{1,0:T(8,128)(2,1)S(1)}, bf16[2,4,16,256,256]{4,3,2,1,0:T(8,128)(2,1)}) custom-call(s32[2,1,16]{2,1,0:T(1,128)S(1)} %copy-done.25, s32[2,1,1024]{2,1,0:T(1,128)S(1)} %copy-done.21, bf16[2048,3072]{1,0:T(8,128)(2,1)S(1)} %copy-done, bf16[2048,3072]{1,0:T(8,128)(2,1)S(1)} %copy-done, bf16[2048,3072]{1,0:T(8,128)(2,1)S(1)} %copy-done, ...), custom_call_target="tpu_custom_call" | custom-call | tf_op jit(solution)/shard_map/attention/pallas_call | solution.py:291
  57.9 2.0 copy-done.13
  59.9 106.6 %feed_forward.1 = (bf16[2,1,1024,1024]{3,2,1,0:T(8,128)(2,1)}, f32[2048,1024]{1,0:T(8,128)}, bf16[2048,1024]{1,0:T(8,128)(2,1)}) custom-call(bf16[2048,1024]{1,0:T(8,128)(2,1)} %copy-done.13, bf16[2,1,1024,1024]{3,2,1,0:T(8,128)(2,1)} %tok_ref.7, bf16[2,1,1024,1024]{3,2,1,0:T(8,128)(2,1)} %cot_ref.1, bf16[1024,1024]{1,0:T(8,128)(2,1)} %wa_ref.1, ...), custom_call_target="tpu_custom_call" | custom-call | tf_op jit(solution)/shard_map/feed_forward/pallas_call | solution.py:370
  166.6 4.6 %copy-done.1 = bf16[2048,3072]{1,0:T(8,128)(2,1)S(1)} copy-done((bf16[2048,3072]{1,0:T(8,128)(2,1)S(1)}, bf16[2048,3072]{1,0:T(8,128)(2,1)}, u32[]{:S(2)}) %copy-start.1) | copy-done | bytes 12582936
  171.1 2.2 copy-done.12
  173.3 49.0 %attention_grad.1 = (bf16[2048,1024]{1,0:T(8,128)(2,1)S(1)}, bf16[2048,1024]{1,0:T(8,128)(2,1)S(1)}, bf16[2048,1024]{1,0:T(8,128)(2,1)S(1)}, f32[64,1024]{1,0:T(8,128)S(1)}, f32[64,1024]{1,0:T(8,128)S(1)}) custom-call(bf16[2048,3072]{1,0:T(8,128)(2,1)S(1)} %copy-done.1, bf16[2048,3072]{1,0:T(8,128)(2,1)S(1)} %copy-done.1, bf16[2048,3072]{1,0:T(8,128)(2,1)S(1)} %copy-done.1, ...), custom_call_target="tpu_custom_call" | custom-call | tf_op jit(solution)/shard_map/attention_grad/pallas_call | solution.py:454
  222.3 2.0 copy-done.6
  224.4 2.0 copy-done.8
  226.4 3.7 %copy-done.7 = bf16[2048,1024]{1,0:T(8,128)(2,1)S(1)} copy-done((bf16[2048,1024]{1,0:T(8,128)(2,1)S(1)}, bf16[2048,1024]{1,0:T(8,128)(2,1)}, u32[]{:S(2)}) %copy-start.7) | copy-done | bytes 4194328
  230.1 2.2 copy-done.9
  232.2 22.4 %grad_first_sum.1 = (bf16[1024,1024]{1,0:T(8,128)(2,1)S(1)}, bf16[16,2048]{1,0:T(8,128)(2,1)S(1)}) custom-call(bf16[2048,1024]{1,0:T(8,128)(2,1)S(1)} %get-tuple-element.34.dq_ref, bf16[2048,1024]{1,0:T(8,128)(2,1)S(1)} %copy-done.7, bf16[2048,1024]{1,0:T(8,128)(2,1)S(1)} %copy-done.9, bf16[2,1,1024,1024]{3,2,1,0:T(8,128)(2,1)S(1)} %copy-done.3, ...), custom_call_target="tpu_custom_call" | custom-call | tf_op jit(solution)/shard_map/grad_first_sum/pallas_call | solution.py:604
  254.7 1.2 copy-done.15
  255.9 17.6 %grad_last.1 = (bf16[2,1,1024,1024]{3,2,1,0:T(8,128)(2,1)}, f32[1,10,1024]{2,1,0:T(8,128)S(1)}, f32[1,1024,512]{2,1,0:T(8,128)}, f32[1,512]{1,0:T(1,128)}, f32[1,512,2048]{2,1,0:T(8,128)}, /*index=5*/f32[1,2048]{1,0:T(1,128)}) custom-call(bf16[2048,1024]{1,0:T(8,128)(2,1)} %copy-done.5, bf16[2048,1024]{1,0:T(8,128)(2,1)} %copy-done.6, ...), custom_call_target="tpu_custom_call" | custom-call | tf_op jit(solution)/shard_map/grad_last/pallas_call | solution.py:722
  (35 shorter events, 1.4 us)
Async XLA Ops:
  0.6 2.2 copy-start.2
  2.8 2.8 %copy-start.4 = (bf16[1024,3072]{1,0:T(8,128)(2,1)S(1)}, bf16[1024,3072]{1,0:T(8,128)(2,1)}, u32[]{:S(2)}) copy-start(bf16[1024,3072]{1,0:T(8,128)(2,1)} %w_ref.5) | copy-start | bytes 18874372
  5.6 1.6 copy-start.10
  7.2 1.2 copy-start.14
  8.4 0.8 copy-start.16
  9.2 0.7 copy-start.18
  9.9 0.7 copy-start.20
  10.6 0.7 copy-start.22
  12.6 18.6 %copy-start.21 = (s32[2,1,1024]{2,1,0:T(1,128)S(1)}, s32[2,1,1024]{2,1,0:T(1,128)}, u32[]{:S(2)}) copy-start(s32[2,1,1024]{2,1,0:T(1,128)} %seg_ref.1) | copy-start | bytes 24580
  12.6 18.6 %copy-start.25 = (s32[2,1,16]{2,1,0:T(1,128)S(1)}, s32[2,1,16]{2,1,0:T(1,128)}, u32[]{:S(2)}) copy-start(s32[2,1,16]{2,1,0:T(1,128)} %task_ref.1) | copy-start | bytes 388
  31.2 4.6 %copy-start = (bf16[2048,3072]{1,0:T(8,128)(2,1)S(1)}, bf16[2048,3072]{1,0:T(8,128)(2,1)}, u32[]{:S(2)}) copy-start(bf16[2048,3072]{1,0:T(8,128)(2,1)} %get-tuple-element.28.q_ref.k_ref.v_ref) | copy-start | bytes 37748740
  57.9 2.0 copy-start.13
  166.6 4.6 %copy-start.1 = (bf16[2048,3072]{1,0:T(8,128)(2,1)S(1)}, bf16[2048,3072]{1,0:T(8,128)(2,1)}, u32[]{:S(2)}) copy-start(bf16[2048,3072]{1,0:T(8,128)(2,1)} %get-tuple-element.28.q_ref.k_ref.v_ref) | copy-start | bytes 37748740
  171.1 2.2 copy-start.12
  173.3 53.0 %copy-start.3 = (bf16[2,1,1024,1024]{3,2,1,0:T(8,128)(2,1)S(1)}, bf16[2,1,1024,1024]{3,2,1,0:T(8,128)(2,1)}, u32[]{:S(2)}) copy-start(bf16[2,1,1024,1024]{3,2,1,0:T(8,128)(2,1)} %tok_ref.7) | copy-start | bytes 12582916
  173.3 53.0 %copy-start.19 = (bf16[1024]{0:T(1024)(128)(2,1)S(1)}, bf16[1024]{0:T(1024)(128)(2,1)}, u32[]{:S(2)}) copy-start(bf16[1024]{0:T(1024)(128)(2,1)} %gain_ref.7) | copy-start | bytes 6148
  222.3 2.0 copy-start.6
  224.3 2.0 copy-start.8
  226.3 28.3 %copy-start.5 = (bf16[2048,1024]{1,0:T(8,128)(2,1)}, bf16[2048,1024]{1,0:T(8,128)(2,1)S(1)}, u32[]{:S(2)}) copy-start(bf16[2048,1024]{1,0:T(8,128)(2,1)S(1)} %get-tuple-element.34.dq_ref) | copy-start | bytes 12582916
  226.3 3.7 %copy-start.7 = (bf16[2048,1024]{1,0:T(8,128)(2,1)S(1)}, bf16[2048,1024]{1,0:T(8,128)(2,1)}, u32[]{:S(2)}) copy-start(bf16[2048,1024]{1,0:T(8,128)(2,1)} %copy-done.6) | copy-start | bytes 12582916
  230.1 2.2 copy-start.9
  232.2 22.4 %copy-start.11 = (bf16[1,512,2048]{2,1,0:T(8,128)(2,1)S(1)}, bf16[1,512,2048]{2,1,0:T(8,128)(2,1)}, u32[]{:S(2)}) copy-start(bf16[1,512,2048]{2,1,0:T(8,128)(2,1)} %wout_ref.1) | copy-start | bytes 6291460
  232.2 22.5 %copy-start.17 = (bf16[1,10,1024]{2,1,0:T(8,128)(2,1)S(1)}, bf16[1,10,1024]{2,1,0:T(8,128)(2,1)}, u32[]{:S(2)}) copy-start(bf16[1,10,1024]{2,1,0:T(8,128)(2,1)} %embed_ref.3) | copy-start | bytes 61444
  254.7 1.2 copy-start.15
  (2 other events, 1.4 us)

commit v2 on v1

v2 whole, which is shorter than its diff:
```python
import functools

import jax
import jax.numpy as jnp
from jax import lax
from jax.experimental import pallas as pl
from jax.experimental.pallas import tpu as pltpu
from jax.sharding import PartitionSpec as P

bf16 = jnp.bfloat16
f32 = jnp.float32

HEADS = 16
HEAD_DIM = 64
GROUP = 4
LANES = GROUP * HEAD_DIM
QB = 64
MOST = 128
WIN = MOST + QB
PAD = 16
EPSILON = 1e-05
NEGATIVE = -1e30
LOG2E = 1.4426950408889634
LN2 = 0.6931471805599453
GELU_A = 0.7978845608028654
GELU_B = 0.044715
VMEM_LIMIT = 62 << 20
CHUNK = 32
QKV_TILE = 256
FF_CHUNK = 1024
MESH = pl.DeviceIdType.MESH


def dot_nn(left, right):
    return jnp.dot(left, right, preferred_element_type=f32)


def dot_nt(left, right):
    return lax.dot_general(
        left, right, (((1,), (1,)), ((), ())), preferred_element_type=f32
    )


def dot_tn(left, right):
    return lax.dot_general(
        left, right, (((0,), (0,)), ((), ())), preferred_element_type=f32
    )


def row_vector(ref, part=slice(None)):
    return ref[part].astype(f32)[None, :]


def normalise(hidden):
    centred = hidden - jnp.mean(hidden, axis=1, keepdims=True)
    spread = jnp.mean(centred * centred, axis=1, keepdims=True)
    inverse = lax.rsqrt(spread + EPSILON)
    return centred * inverse, inverse


def norm_backward(grad, gain, unit, inverse):
    scaled = grad * gain
    mean_one = jnp.mean(scaled, axis=1, keepdims=True)
    mean_two = jnp.mean(scaled * unit, axis=1, keepdims=True)
    return inverse * (scaled - mean_one - unit * mean_two)


def gelu_both(value, grad):
    square = value * value
    half = 0.5 + 0.5 * jnp.tanh(value * (GELU_A + (GELU_A * GELU_B) * square))
    act = value * half
    slope = half + (act * (2 * GELU_A + (6 * GELU_A * GELU_B) * square)) * (1.0 - half)
    return act.astype(bf16), (grad * slope).astype(bf16)


def barrier_with(peers):
    barrier = pltpu.get_barrier_semaphore()
    for peer in peers:
        pl.semaphore_signal(barrier, inc=1, device_id=peer, device_id_type=MESH)
    return barrier


def qkv_kernel(
    tasks,
    tok_ref,
    gain_ref,
    shift_ref,
    w_hbm,
    b_ref,
    embed_ref,
    win_hbm,
    bin_ref,
    wout_hbm,
    bout_ref,
    *refs,
):
    count = (len(refs) - 13) // 2
    weights_hbm = refs[:count]
    mixed_ref, hidden_ref, states_ref = refs[count : count + 3]
    weights = refs[count + 3 : 2 * count + 3]
    (
        win,
        wout,
        padded,
        own,
        gathered,
        w_ref,
        current,
        load_sem,
        send_sem,
        recv_sem,
    ) = refs[2 * count + 3 :]
    step = pl.program_id(0)
    last = pl.num_programs(0) - 1
    row_axis = lax.axis_index("batch")
    me = lax.axis_index("task")
    peers = [(row_axis, lax.rem(me + k, tasks)) for k in range(1, tasks)]

    width = tok_ref.shape[1]

    copies = [(w_hbm, w_ref), (win_hbm.at[0], win), (wout_hbm.at[0], wout)]
    copies += list(zip(weights_hbm, weights))

    def load(index):
        return pltpu.make_async_copy(*copies[index], load_sem.at[index])

    def send(k):
        return pltpu.make_async_remote_copy(
            src_ref=own,
            dst_ref=gathered.at[me],
            send_sem=send_sem.at[k - 1],
            recv_sem=recv_sem.at[k - 1],
            device_id=peers[k - 1],
            device_id_type=MESH,
        )

    def norm():
        normed, _ = normalise(tok_ref[...].astype(f32))
        return (normed * row_vector(gain_ref) + row_vector(shift_ref)).astype(bf16)

    @pl.when(step == 0)
    def _():
        load(0).start()
        barrier_with(peers)
        current[...] = norm()
        load(0).wait()
        for index in range(1, len(copies)):
            load(index).start()

    @pl.when(step == 2)
    def _():
        load(1).wait()
        load(2).wait()
        padded[...] = jnp.zeros(padded.shape, f32)
        padded[: embed_ref.shape[1], :] = embed_ref[0].astype(f32)
        pre = dot_nn(padded[...].astype(bf16), win[...]) + bin_ref[...].astype(f32)
        hidden = jnp.tanh(pre)
        hidden_ref[...] = hidden
        states = dot_nn(hidden.astype(bf16), wout[...]) + bout_ref[...].astype(f32)
        states = states.astype(bf16)
        own[...] = states
        gathered[me] = states
        pl.semaphore_wait(pltpu.get_barrier_semaphore(), tasks - 1)
        for k in range(1, tasks):
            send(k).start()

    @pl.when(step > 0)
    def _():
        mixed = dot_nn(current[...], w_ref[...]) + row_vector(b_ref)
        following = norm()
        mixed_ref[:, :width] = (mixed[:, :width] * (HEAD_DIM ** (-0.5) * LOG2E)).astype(bf16)
        mixed_ref[:, width:] = mixed[:, width:].astype(bf16)
        current[...] = following

    @pl.when(step == last)
    def _():
        for k in range(1, tasks):
            send(k).wait()
        states_ref[...] = gathered[...].reshape(states_ref.shape)
        for index in range(3, len(copies)):
            load(index).wait()


def qkv_call(tasks, tokens, gain, shift, w_qkv, b_qkv, embed, w_in, b_in, w_out, b_out, keep):
    micro, rows, seq, width = tokens.shape
    tile = QKV_TILE
    per_row = seq // tile
    rank = w_in.shape[2]
    whole1 = lambda x: pl.BlockSpec(x.shape, lambda i: (0,) * x.ndim)
    tiles = micro * rows * per_row
    ahead = lambda i: jnp.minimum(i, tiles - 1)
    return pl.pallas_call(
        functools.partial(qkv_kernel, tasks),
        grid=(tiles + 1,),
        in_specs=[
            pl.BlockSpec(
                (None, None, tile, width),
                lambda i: (
                    ahead(i) // (rows * per_row),
                    lax.rem(ahead(i) // per_row, rows),
                    lax.rem(ahead(i), per_row),
                    0,
                ),
            ),
            whole1(gain),
            whole1(shift),
            pl.BlockSpec(memory_space=pl.ANY),
            whole1(b_qkv),
            whole1(embed),
            pl.BlockSpec(memory_space=pl.ANY),
            whole1(b_in),
            pl.BlockSpec(memory_space=pl.ANY),
            whole1(b_out),
        ]
        + [pl.BlockSpec(memory_space=pl.ANY)] * len(keep),
        out_specs=[
            pl.BlockSpec((tile, 3 * width), lambda i: (jnp.maximum(i - 1, 0), 0)),
            pl.BlockSpec((PAD, rank), lambda i: (0, 0)),
            pl.BlockSpec((tasks * PAD, 2 * width), lambda i: (0, 0)),
        ]
        + [pl.BlockSpec(memory_space=pltpu.VMEM)] * len(keep),
        out_shape=[
            jax.ShapeDtypeStruct((micro * rows * seq, 3 * width), bf16),
            jax.ShapeDtypeStruct((PAD, rank), f32),
            jax.ShapeDtypeStruct((tasks * PAD, 2 * width), bf16),
        ]
        + [pltpu.VMEM(x.shape, bf16) for x in keep],
        scratch_shapes=[
            pltpu.VMEM(w_in.shape[1:], bf16),
            pltpu.VMEM(w_out.shape[1:], bf16),
            pltpu.VMEM((PAD, width), f32),
            pltpu.VMEM((PAD, 2 * width), bf16),
            pltpu.VMEM((tasks, PAD, 2 * width), bf16),
            pltpu.VMEM(w_qkv.shape, bf16),
            pltpu.VMEM((tile, width), bf16),
            pltpu.SemaphoreType.DMA((3 + len(keep),)),
            pltpu.SemaphoreType.DMA((tasks - 1,)),
            pltpu.SemaphoreType.DMA((tasks - 1,)),
        ],
        compiler_params=pltpu.CompilerParams(
            collective_id=0, has_side_effects=True, vmem_limit_bytes=VMEM_LIMIT
        ),
        name="norm_qkv",
    )(tokens, gain, shift, w_qkv, b_qkv, embed, w_in, b_in, w_out, b_out, *keep)


def stack_heads(block):
    lane = lax.broadcasted_iota(jnp.int32, (QB, 128), 1)
    zero = jnp.zeros((QB, 128), block.dtype)
    rows = []
    for h in range(GROUP):
        part = jnp.where((lane < HEAD_DIM) == (h % 2 == 0), block[:, (h // 2) * 128 :][:, :128], zero)
        rows.append(jnp.concatenate([part, zero] if h < 2 else [zero, part], axis=1))
    return jnp.concatenate(rows, axis=0)


def pick_heads(stacked):
    lane = lax.broadcasted_iota(jnp.int32, (QB, 128), 1)
    low = jnp.where(lane < HEAD_DIM, stacked[:QB, :128], stacked[QB : 2 * QB, :128])
    high = jnp.where(lane < HEAD_DIM, stacked[2 * QB : 3 * QB, 128:], stacked[3 * QB :, 128:])
    return jnp.concatenate([low, high], axis=1)


def fill_mask(seg_ref, task_ref, micro, prefix, bias, by_key):
    segments = seg_ref[...]
    seq = segments.shape[1]
    token_task = jnp.zeros(segments.shape, jnp.int32)
    for s in range(task_ref.shape[-1]):
        token_task = jnp.where(segments == s, task_ref[micro, 0, s], token_task)
    segments = segments.astype(f32)
    for c in range(0, seq, 128):
        by_key[c : c + 128, :] = jnp.broadcast_to(segments[:, c : c + 128], (128, 128)).T
    for b in range(seq // QB):
        start = max(b * QB - MOST, 0)

        def twice(x):
            part = x[:, b * QB : (b + 1) * QB]
            return jnp.concatenate([part, part], axis=1)

        key_pos = start + lax.broadcasted_iota(jnp.int32, (WIN, 128), 0)
        query_pos = b * QB + (lax.broadcasted_iota(jnp.int32, (WIN, 128), 1) & (QB - 1))
        own = (by_key[start : start + WIN, :] == twice(segments)) & (key_pos <= query_pos)
        bias[b, :WIN, :] = jnp.where(own, 0.0, NEGATIVE)
        index = lax.broadcasted_iota(jnp.int32, (bias.shape[1] - WIN, 128), 0)
        fits = (lax.shift_right_logical(index, 4) == twice(token_task)) & (
            (index & (PAD - 1)) < prefix
        )
        bias[b, WIN:, :] = jnp.where(fits, 0.0, NEGATIVE)


def own_window(block):
    start = max(block * QB - MOST, 0)
    return slice(start, start + WIN)


def fold_rows(part, combine):
    return combine(part.reshape(part.shape[0] // 8, 8, part.shape[1]), axis=0)


def skewed(items, *stages):
    for step in range(len(items) + len(stages) - 1):
        for delay, stage in enumerate(stages):
            if 0 <= step - delay < len(items):
                stage(step - delay, *items[step - delay])


def attention_kernel(
    prefix,
    task_ref,
    seg_ref,
    q_ref,
    k_ref,
    v_ref,
    pk_ref,
    pv_ref,
    *refs,
):
    out_ref, probs_ref, bias, by_key, work = refs
    micro = pl.program_id(0)

    @pl.when(pl.program_id(1) == 0)
    def _():
        fill_mask(seg_ref, task_ref, micro, prefix, bias, by_key)

    height = work.shape[1]
    pieces = [slice(c, c + CHUNK) for c in range(0, height, CHUNK)]

    def scores(index, group, block):
        lanes = slice(group * LANES, (group + 1) * LANES)
        keys = jnp.concatenate([k_ref[own_window(block), lanes], pk_ref[:, lanes]], axis=0)
        queries = stack_heads(q_ref[block * QB : (block + 1) * QB, lanes])
        work[index % 2] = dot_nt(keys, queries)

    def softmax(index, group, block):
        slot = work.at[index % 2]
        top = None
        for piece in pieces:
            hidden = bias[block, piece, :]
            part = slot[piece, :] + jnp.concatenate([hidden, hidden], axis=1)
            slot[piece, :] = part
            part = fold_rows(part, jnp.max)
            top = part if top is None else jnp.maximum(top, part)
        top = jnp.max(top, axis=0, keepdims=True)
        total = None
        for piece in pieces:
            part = jnp.exp2(slot[piece, :] - top)
            slot[piece, :] = part
            part = fold_rows(part, jnp.sum)
            total = part if total is None else total + part
        inverse = 1.0 / jnp.sum(total, axis=0, keepdims=True)
        for piece in pieces:
            probs_ref[group, block, piece, :] = (slot[piece, :] * inverse).astype(bf16)

    def attend(index, group, block):
        lanes = slice(group * LANES, (group + 1) * LANES)
        values = jnp.concatenate([v_ref[own_window(block), lanes], pv_ref[:, lanes]], axis=0)
        result = pick_heads(dot_tn(probs_ref[group, block], values))
        out_ref[block * QB : (block + 1) * QB, lanes] = result.astype(bf16)

    items = [
        (group, block)
        for group in range(q_ref.shape[1] // LANES)
        for block in range(q_ref.shape[0] // QB)
    ]
    skewed(items, scores, softmax, attend)


def attention_call(mixed, segments, tasks, states, prefix):
    micro, _, seq = segments.shape
    width = mixed.shape[1] // 3
    groups = width // LANES
    blocks = seq // QB
    keys = WIN + states.shape[0]
    both = 2
    steps = groups // both
    part = lambda offset: pl.BlockSpec((seq, both * LANES), lambda r, g: (r, offset + g))
    piece = lambda offset: pl.BlockSpec(
        (states.shape[0], both * LANES), lambda r, g: (0, offset + g)
    )
    return pl.pallas_call(
        functools.partial(attention_kernel, prefix),
        grid=(micro, steps),
        in_specs=[
            pl.BlockSpec(memory_space=pltpu.SMEM),
            pl.BlockSpec((None, 1, seq), lambda r, g: (r, 0, 0)),
            part(0),
            part(steps),
            part(2 * steps),
            piece(0),
            piece(steps),
        ],
        out_specs=[
            part(0),
            pl.BlockSpec((None, both, blocks, keys, LANES), lambda r, g: (r, g, 0, 0, 0)),
        ],
        out_shape=[
            jax.ShapeDtypeStruct((micro * seq, width), bf16),
            jax.ShapeDtypeStruct((micro, groups, blocks, keys, LANES), bf16),
        ],
        scratch_shapes=[
            pltpu.VMEM((blocks, keys, 128), f32),
            pltpu.VMEM((seq, 128), f32),
            pltpu.VMEM((2, keys, LANES), f32),
        ],
        compiler_params=pltpu.CompilerParams(vmem_limit_bytes=VMEM_LIMIT),
        name="attention",
    )(tasks, segments, mixed, mixed, mixed, states, states)


def mlp_kernel(
    att_ref,
    tok_ref,
    cot_ref,
    wa_ref,
    ba_ref,
    gain_ref,
    shift_ref,
    wf_ref,
    bf_ref,
    wp_ref,
    bp_ref,
    out_ref,
    gres_ref,
    gatt_ref,
    act_all,
    gpre_all,
):
    gain = row_vector(gain_ref)
    resid = tok_ref[...].astype(f32) + dot_nn(att_ref[...], wa_ref[...]) + row_vector(ba_ref)
    unit, inverse = normalise(resid)
    normed = (unit * gain + row_vector(shift_ref)).astype(bf16)
    grad_out = cot_ref[...]
    for start in range(0, wf_ref.shape[1], FF_CHUNK):
        part = slice(start, start + FF_CHUNK)
        pre = dot_nn(normed, wf_ref[:, part]) + row_vector(bf_ref, part)
        act, gpre = gelu_both(pre, dot_nt(grad_out, wp_ref[part, :]))
        act_all[:, part] = act
        gpre_all[:, part] = gpre
    grad_normed = dot_nt(gpre_all[...], wf_ref[...])
    out = resid + dot_nn(act_all[...], wp_ref[...]) + row_vector(bp_ref)
    out_ref[...] = out.astype(bf16)
    grad_resid = grad_out.astype(f32) + norm_backward(grad_normed, gain, unit, inverse)
    grad_branch = grad_resid.astype(bf16)
    gres_ref[...] = grad_branch
    gatt_ref[...] = dot_nt(grad_branch, wa_ref[...]).astype(bf16)


def mlp_call(attended, tokens, cotangent, w_attn, b_attn, gain, shift, w_fc, b_fc, w_proj, b_proj):
    micro, rows, seq, width = tokens.shape
    tile = 256
    per_row = seq // tile
    flat = pl.BlockSpec((tile, width), lambda i: (i, 0))
    deep = pl.BlockSpec(
        (None, None, tile, width),
        lambda i: (i // (rows * per_row), (i // per_row) % rows, i % per_row, 0),
    )
    once = lambda x: pl.BlockSpec(
        x.shape, lambda i: (0,) * x.ndim, pipeline_mode=pl.Buffered(1)
    )
    weights = (w_attn, b_attn, gain, shift, w_fc, b_fc, w_proj, b_proj)
    count = micro * rows * seq
    return pl.pallas_call(
        mlp_kernel,
        grid=(count // tile,),
        in_specs=[flat, deep, deep] + [once(x) for x in weights],
        out_specs=[deep, flat, flat],
        out_shape=[
            jax.ShapeDtypeStruct(tokens.shape, bf16),
            jax.ShapeDtypeStruct((count, width), bf16),
            jax.ShapeDtypeStruct((count, width), bf16),
        ],
        scratch_shapes=[pltpu.VMEM((tile, w_fc.shape[1]), bf16)] * 2,
        compiler_params=pltpu.CompilerParams(vmem_limit_bytes=VMEM_LIMIT),
        name="feed_forward",
    )(attended, tokens, cotangent, *weights)


def attention_grad_kernel(
    q_ref,
    k_ref,
    v_ref,
    pk_ref,
    pv_ref,
    probs_ref,
    g_ref,
    dq_ref,
    dk_ref,
    dv_ref,
    dpk_ref,
    dpv_ref,
    key_sum,
    value_sum,
    prefix_key_sum,
    prefix_value_sum,
    work,
    score_grad,
):
    blocks = q_ref.shape[0] // QB
    pieces = [slice(c, c + CHUNK) for c in range(0, work.shape[1], CHUNK)]

    def prob_grads(index, block):
        values = jnp.concatenate([v_ref[own_window(block), :], pv_ref[...]], axis=0)
        grads = stack_heads(g_ref[block * QB : (block + 1) * QB, :])
        work[index % 2] = dot_nt(values, grads)

    def softmax_grads(index, block):
        slot = work.at[index % 2]
        delta = None
        for piece in pieces:
            part = slot[piece, :] * probs_ref[block, piece, :].astype(f32)
            slot[piece, :] = part
            part = fold_rows(part, jnp.sum)
            delta = part if delta is None else delta + part
        delta = jnp.sum(delta, axis=0, keepdims=True)
        for piece in pieces:
            part = slot[piece, :] - probs_ref[block, piece, :].astype(f32) * delta
            score_grad[index % 2, piece, :] = part.astype(bf16)

    def mixed_grads(index, block):
        rows = slice(block * QB, (block + 1) * QB)
        window = own_window(block)
        keys = jnp.concatenate([k_ref[window, :], pk_ref[...]], axis=0)
        back = score_grad[index % 2]
        dv = dot_nn(probs_ref[block], stack_heads(g_ref[rows, :]))
        dk = dot_nn(back, stack_heads(q_ref[rows, :]))
        dq = pick_heads(dot_tn(back, keys))
        dq_ref[rows, :] = (dq * HEAD_DIM ** (-0.5)).astype(bf16)
        start = window.start
        old = 0 if block == 0 else block * QB - start if start else WIN
        for total, fresh in ((key_sum, dk), (value_sum, dv)):
            if old:
                total[start : start + old, :] += fresh[:old]
            if old < WIN:
                total[start + old : start + WIN, :] = fresh[old:WIN]
        for total, fresh in ((prefix_key_sum, dk), (prefix_value_sum, dv)):
            if block == 0:
                total[...] = fresh[WIN:]
            else:
                total[...] += fresh[WIN:]
        done = slice(start, window.stop if block == blocks - 1 else start + QB if block >= 2 else 0)
        if done.stop > done.start:
            dk_ref[done, :] = (key_sum[done, :] * LN2).astype(bf16)
            dv_ref[done, :] = value_sum[done, :].astype(bf16)

    skewed([(block,) for block in range(blocks)], prob_grads, softmax_grads, mixed_grads)

    @pl.when(pl.program_id(1) == 0)
    def _():
        dpk_ref[...] = prefix_key_sum[...] * LN2
        dpv_ref[...] = prefix_value_sum[...]

    @pl.when(pl.program_id(1) != 0)
    def _():
        dpk_ref[...] += prefix_key_sum[...] * LN2
        dpv_ref[...] += prefix_value_sum[...]


def attention_grad_call(mixed, states, probs, grad_attended):
    micro, groups, blocks, keys, _ = probs.shape
    seq = blocks * QB
    width = grad_attended.shape[1]
    prefix_rows = states.shape[0]
    part = lambda offset: pl.BlockSpec((seq, LANES), lambda g, r: (r, offset + g))
    piece = lambda offset: pl.BlockSpec((prefix_rows, LANES), lambda g, r: (0, offset + g))
    return pl.pallas_call(
        attention_grad_kernel,
        grid=(groups, micro),
        in_specs=[
            part(0),
            part(groups),
            part(2 * groups),
            piece(0),
            piece(groups),
            pl.BlockSpec((None, None, blocks, keys, LANES), lambda g, r: (r, g, 0, 0, 0)),
            part(0),
        ],
        out_specs=[part(0)] * 3 + [piece(0)] * 2,
        out_shape=[jax.ShapeDtypeStruct((micro * seq, width), bf16)] * 3
        + [jax.ShapeDtypeStruct((prefix_rows, width), f32)] * 2,
        scratch_shapes=[pltpu.VMEM((seq, LANES), f32)] * 2
        + [pltpu.VMEM((prefix_rows, LANES), f32)] * 2
        + [pltpu.VMEM((2, keys, LANES), f32), pltpu.VMEM((2, keys, LANES), bf16)],
        compiler_params=pltpu.CompilerParams(vmem_limit_bytes=VMEM_LIMIT),
        name="attention_grad",
    )(mixed, mixed, mixed, states, states, probs, grad_attended)


def sum_kernel(
    tasks,
    shards,
    dq_ref,
    dk_ref,
    dv_ref,
    tok_ref,
    gres_ref,
    gain_ref,
    w_hbm,
    dpk_ref,
    dpv_ref,
    grad_ref,
    summed_ref,
    w_ref,
    send_a,
    recv_a,
    send_b,
    recv_b,
    gathered,
    load_sem,
    sems,
    sems_b,
):
    step = pl.program_id(0)
    last = pl.num_programs(0) - 1
    shard = lax.axis_index("batch")
    task = lax.axis_index("task")
    task_peers = [(shard, lax.rem(task + k, tasks)) for k in range(1, tasks)]
    shard_peers = [(lax.rem(shard + k, shards), task) for k in range(1, shards)]
    width = dpk_ref.shape[1]
    lanes = send_b.shape[2]
    load = pltpu.make_async_copy(w_hbm, w_ref, load_sem)

    def to_task(k):
        return pltpu.make_async_remote_copy(
            src_ref=send_a.at[lax.rem(task + k, tasks)],
            dst_ref=recv_a.at[k - 1],
            send_sem=sems.at[0, k - 1],
            recv_sem=sems.at[1, k - 1],
            device_id=task_peers[k - 1],
            device_id_type=MESH,
        )

    def to_shard(k):
        return pltpu.make_async_remote_copy(
            src_ref=send_b.at[lax.rem(shard + k, shards)],
            dst_ref=recv_b.at[k - 1],
            send_sem=sems_b.at[0, k - 1],
            recv_sem=sems_b.at[1, k - 1],
            device_id=shard_peers[k - 1],
            device_id_type=MESH,
        )

    def back_to_shard(k):
        return pltpu.make_async_remote_copy(
            src_ref=gathered.at[shard],
            dst_ref=gathered.at[shard],
            send_sem=sems_b.at[2, k - 1],
            recv_sem=sems_b.at[3, k - 1],
            device_id=shard_peers[k - 1],
            device_id_type=MESH,
        )

    def start_tasks():
        pl.semaphore_wait(pltpu.get_barrier_semaphore(), tasks - 1 + shards - 1)
        for k in range(1, tasks):
            to_task(k).start()

    def start_shards():
        for k in range(1, tasks):
            to_task(k).wait()
        total = send_a[task].astype(f32)
        for k in range(1, tasks):
            total = total + recv_a[k - 1].astype(f32)
        total = total.astype(bf16)
        for c in range(shards):
            send_b[c] = total[:, c * lanes : (c + 1) * lanes]
        for k in range(1, shards):
            to_shard(k).start()

    def start_back():
        for k in range(1, shards):
            to_shard(k).wait()
        total = send_b[shard].astype(f32)
        for k in range(1, shards):
            total = total + recv_b[k - 1].astype(f32)
        gathered[shard] = total.astype(bf16)
        for k in range(1, shards):
            back_to_shard(k).start()

    @pl.when(step == 0)
    def _():
        load.start()
        barrier_with(task_peers + shard_peers)
        for t in range(tasks):
            part = slice(t * PAD, (t + 1) * PAD)
            send_a[t, :, :width] = dpk_ref[part, :].astype(bf16)
            send_a[t, :, width:] = dpv_ref[part, :].astype(bf16)
        load.wait()

    @pl.when(step == 1)
    def _():
        start_tasks()

    @pl.when(step == 2)
    def _():
        start_shards()

    @pl.when(step == 3)
    def _():
        start_back()

    grad = dot_nt(dq_ref[...], w_ref[:, :width])
    grad = grad + dot_nt(dk_ref[...], w_ref[:, width : 2 * width])
    grad = grad + dot_nt(dv_ref[...], w_ref[:, 2 * width :])
    unit, inverse = normalise(tok_ref[...].astype(f32))
    back = norm_backward(grad, row_vector(gain_ref), unit, inverse)
    grad_ref[...] = (gres_ref[...].astype(f32) + back).astype(bf16)

    @pl.when(step == last)
    def _():
        for k in range(1, shards):
            back_to_shard(k).wait()
        for c in range(shards):
            summed_ref[:, c * lanes : (c + 1) * lanes] = gathered[c]


def sum_call(tasks, shards, tiles, tile, dq, dk, dv, tokens, grad_resid, gain, w_qkv, dpk, dpv):
    seq, width = tokens.shape[2:]
    per_row = seq // tile
    assert tiles >= 4
    flat = pl.BlockSpec((tile, width), lambda i: (i, 0))
    lanes = 2 * width // shards
    whole = lambda x: pl.BlockSpec(x.shape, lambda i: (0,) * x.ndim)
    return pl.pallas_call(
        functools.partial(sum_kernel, tasks, shards),
        grid=(tiles,),
        in_specs=[flat, flat, flat]
        + [
            pl.BlockSpec((None, None, tile, width), lambda i: (i // per_row, 0, i % per_row, 0)),
            flat,
            whole(gain),
            pl.BlockSpec(memory_space=pl.ANY),
            whole(dpk),
            whole(dpv),
        ],
        out_specs=[flat, pl.BlockSpec((PAD, 2 * width), lambda i: (0, 0))],
        out_shape=[
            jax.ShapeDtypeStruct((tiles * tile, width), bf16),
            jax.ShapeDtypeStruct((PAD, 2 * width), bf16),
        ],
        scratch_shapes=[
            pltpu.VMEM(w_qkv.shape, bf16),
            pltpu.VMEM((tasks, PAD, 2 * width), bf16),
            pltpu.VMEM((tasks - 1, PAD, 2 * width), bf16),
            pltpu.VMEM((shards, PAD, lanes), bf16),
            pltpu.VMEM((shards - 1, PAD, lanes), bf16),
            pltpu.VMEM((shards, PAD, lanes), bf16),
            pltpu.SemaphoreType.DMA,
            pltpu.SemaphoreType.DMA((2, tasks - 1)),
            pltpu.SemaphoreType.DMA((4, shards - 1)),
        ],
        compiler_params=pltpu.CompilerParams(
            collective_id=1, has_side_effects=True, vmem_limit_bytes=VMEM_LIMIT
        ),
        name="grad_first_sum",
    )(dq, dk, dv, tokens, grad_resid, gain, w_qkv, dpk, dpv)


def last_kernel(
    grad_hbm,
    summed_ref,
    hidden_ref,
    embed_ref,
    win_hbm,
    wout_hbm,
    out_hbm,
    gembed_ref,
    gin_hbm,
    gbin_ref,
    gout_hbm,
    gbout_ref,
    win_ref,
    wout_ref,
    held,
    padded,
    gin,
    gout,
    sems,
):
    seq = out_hbm.shape[2]
    load_in = pltpu.make_async_copy(win_hbm.at[0], win_ref, sems.at[0])
    load_out = pltpu.make_async_copy(wout_hbm.at[0], wout_ref, sems.at[1])
    put_in = pltpu.make_async_copy(gin, gin_hbm.at[0], sems.at[2])
    put_out = pltpu.make_async_copy(gout, gout_hbm.at[0], sems.at[3])
    takes, puts = [], []
    for index in range(out_hbm.shape[0]):
        rows = pl.ds(index * seq, seq)
        takes.append(
            pltpu.make_async_copy(grad_hbm.at[rows, :], held.at[rows, :], sems.at[4 + 2 * index])
        )
        puts.append(
            pltpu.make_async_copy(held.at[rows, :], out_hbm.at[index, 0], sems.at[5 + 2 * index])
        )
    for load in [load_out, load_in] + takes:
        load.start()
    summed = summed_ref[...]
    hidden = hidden_ref[...]
    gout[...] = dot_tn(hidden.astype(bf16), summed)
    put_out.start()
    gbout_ref[...] = jnp.sum(summed.astype(f32), axis=0, keepdims=True)
    padded[...] = jnp.zeros(padded.shape, f32)
    padded[: embed_ref.shape[1], :] = embed_ref[0].astype(f32)
    load_out.wait()
    load_in.wait()
    grad_hidden = dot_nt(summed, wout_ref[...])
    for take, put in zip(takes, puts):
        take.wait()
        put.start()
    grad_pre = (grad_hidden * (1.0 - hidden * hidden)).astype(bf16)
    gin[...] = dot_tn(padded[...].astype(bf16), grad_pre)
    put_in.start()
    gbin_ref[...] = jnp.sum(grad_pre.astype(f32), axis=0, keepdims=True)
    gembed_ref[:, 0, :] = dot_nt(grad_pre, win_ref[...])[: embed_ref.shape[1], :]
    for copy in puts + [put_in, put_out]:
        copy.wait()


def last_call(grad, shape, summed, hidden, embed, w_in, w_out):
    width = shape[3]
    anywhere = pl.BlockSpec(memory_space=pl.ANY)
    whole = lambda shape: pl.BlockSpec(shape, lambda i: (0,) * len(shape))
    rank = w_in.shape[2]
    prefix = embed.shape[1]
    return pl.pallas_call(
        last_kernel,
        grid=(1,),
        in_specs=[anywhere]
        + [whole(x.shape) for x in (summed, hidden, embed)]
        + [anywhere, anywhere],
        out_specs=[
            anywhere,
            whole((prefix, 1, width)),
            anywhere,
            whole((1, rank)),
            anywhere,
            whole((1, 2 * width)),
        ],
        out_shape=[
            jax.ShapeDtypeStruct(shape, bf16),
            jax.ShapeDtypeStruct((prefix, 1, width), f32),
            jax.ShapeDtypeStruct(w_in.shape, f32),
            jax.ShapeDtypeStruct((1, rank), f32),
            jax.ShapeDtypeStruct(w_out.shape, f32),
            jax.ShapeDtypeStruct((1, 2 * width), f32),
        ],
        scratch_shapes=[
            pltpu.VMEM(w_in.shape[1:], bf16),
            pltpu.VMEM(w_out.shape[1:], bf16),
            pltpu.VMEM(grad.shape, bf16),
            pltpu.VMEM((PAD, width), f32),
            pltpu.VMEM(w_in.shape[1:], f32),
            pltpu.VMEM(w_out.shape[1:], f32),
            pltpu.SemaphoreType.DMA((4 + 2 * shape[0],)),
        ],
        compiler_params=pltpu.CompilerParams(vmem_limit_bytes=VMEM_LIMIT),
        name="grad_last",
    )(grad, summed, hidden, embed, w_in, w_out)


def on_device(
    tasks,
    shards,
    tokens,
    cotangent,
    segment_ids,
    task_ids,
    ln1_gain,
    ln1_bias,
    w_qkv,
    b_qkv,
    w_attn_out,
    b_attn_out,
    ln2_gain,
    ln2_bias,
    w_fc,
    b_fc,
    w_proj,
    b_proj,
    prefix_embed,
    reparam_in,
    reparam_in_bias,
    reparam_out,
    reparam_out_bias,
):
    mixed, hidden, states, *kept = qkv_call(
        tasks,
        tokens,
        ln1_gain,
        ln1_bias,
        w_qkv,
        b_qkv,
        prefix_embed,
        reparam_in,
        reparam_in_bias,
        reparam_out,
        reparam_out_bias,
        (),
    )
    attended, probs = attention_call(
        mixed, segment_ids, task_ids, states, prefix_embed.shape[1]
    )
    block_out, grad_resid, grad_attended = mlp_call(
        attended,
        tokens,
        cotangent,
        w_attn_out,
        b_attn_out,
        ln2_gain,
        ln2_bias,
        w_fc,
        b_fc,
        w_proj,
        b_proj,
    )
    dq, dk, dv, dpk, dpv = attention_grad_call(mixed, states, probs, grad_attended)
    tile = 512
    first, summed = sum_call(
        tasks,
        shards,
        dq.shape[0] // tile,
        tile,
        dq,
        dk,
        dv,
        tokens,
        grad_resid,
        ln1_gain,
        w_qkv,
        dpk,
        dpv,
    )
    input_grad, gembed, gin, gbin, gout, gbout = last_call(
        first, tokens.shape, summed, hidden, prefix_embed, reparam_in, reparam_out
    )
    return (block_out, input_grad, jnp.swapaxes(gembed, 0, 1), gin, gbin, gout, gbout)


def solution(mesh):
    split = ("batch", "task")
    in_specs = (
        (P(None, split, None, None),) * 2
        + (P(None, split, None),) * 2
        + (P(),) * 12
        + (
            P("task", None, None),
            P("task", None, None),
            P("task", None),
            P("task", None, None),
            P("task", None),
        )
    )
    out_specs = (
        P(None, split, None, None),
        P(None, split, None, None),
        P("task", None, None),
        P("task", None, None),
        P("task", None),
        P("task", None, None),
        P("task", None),
    )
    return jax.shard_map(
        functools.partial(on_device, mesh.shape["task"], mesh.shape["batch"]),
        mesh=mesh,
        in_specs=in_specs,
        out_specs=out_specs,
        check_vma=False,
    )
```

time: 274 us -> 202 us (0.74)
  local copies, waits for them, and re-layouts: 37.1 us -> 0 us
  Pallas kernels: 236 us -> 201 us
    unnamed x53 -> x0, local copies, waits for them, and re-layouts: 37.1 us -> none
    pallas_call x1, Pallas kernels: 49 us -> 26.9 us  [attention_grad_call(): pl.pallas_call(attention_grad_kernel, grid=(groups, micro), in_specs=[par...]
    pallas_call x1, Pallas kernels: 107 us -> 96.7 us  [mlp_call(): pl.pallas_call(mlp_kernel, grid=(count // tile,), in_specs=[flat, deep, d...]
    pallas_call x1, Pallas kernels: 22.1 us -> 18.9 us  [attention_call(): pl.pallas_call(functools.partial(attention_kernel, prefix), grid=(micro,...]
where the time goes in v2:
time: 202 us
  Pallas kernels  201 us (100%)
    pallas_call x1, Pallas kernels, mlp_call(): pl.pallas_call(mlp_kernel, grid=(count // tile,), in_specs=[flat, deep, d...  96.7 us
    pallas_call x1, Pallas kernels, sum_call(): pl.pallas_call(functools.partial(sum_kernel, tasks, shards), grid=(tiles,...  28.6 us
    pallas_call x1, Pallas kernels, attention_grad_call(): pl.pallas_call(attention_grad_kernel, grid=(groups, micro), in_specs=[par...  26.9 us
    pallas_call x1, Pallas kernels, qkv_call(): pl.pallas_call(functools.partial(qkv_kernel, tasks), grid=(tiles + 1,), i...  21.6 us
    pallas_call x1, Pallas kernels, attention_call(): pl.pallas_call(functools.partial(attention_kernel, prefix), grid=(micro,...  18.9 us
    pallas_call x1, Pallas kernels, last_call(): pl.pallas_call(last_kernel, grid=(1,), in_specs=[anywhere] + [whole(x.sha...  8.31 us

profile of v2, /device:TPU:0, one launch (start us, length us, event | category | flops | bytes accessed | tf_op | source)
XLA Modules:
  0.0 202.0 jit_solution(4831766016595986946)
XLA Ops:
  0.6 21.6 %norm_qkv.1 = (bf16[2048,3072]{1,0:T(8,128)(2,1)}, f32[16,512]{1,0:T(8,128)}, bf16[64,2048]{1,0:T(8,128)(2,1)}) custom-call(bf16[2,1,1024,1024]{3,2,1,0:T(8,128)(2,1)} %tok_ref.5, bf16[1024]{0:T(1024)(128)(2,1)} %gain_ref.5, bf16[1024]{0:T(1024)(128)(2,1)} %shift_ref.2, bf16[1024,3072]{1,0:T(8,128)(2,1)} %w_hbm.3, bf16[3072]{0:T(1024)(128)(2,1)} %b_ref.1, ...), custom_call_target="tpu_custom_call" | custom-call | tf_op jit(solution)/shard_map/norm_qkv/pallas_call | solution.py:192
  22.3 18.9 %attention.1 = (bf16[2048,1024]{1,0:T(8,128)(2,1)}, bf16[2,4,16,256,256]{4,3,2,1,0:T(8,128)(2,1)}) custom-call(s32[2,1,16]{2,1,0:T(1,128)} %task_ref.1, s32[2,1,1024]{2,1,0:T(1,128)} %seg_ref.1, bf16[2048,3072]{1,0:T(8,128)(2,1)} %get-tuple-element.28.q_ref.k_ref.v_ref, bf16[2048,3072]{1,0:T(8,128)(2,1)} %get-tuple-element.28.q_ref.k_ref.v_ref, ...), custom_call_target="tpu_custom_call" | custom-call | tf_op jit(solution)/shard_map/attention/pallas_call | solution.py:380
  41.2 96.7 %feed_forward.1 = (bf16[2,1,1024,1024]{3,2,1,0:T(8,128)(2,1)}, bf16[2048,1024]{1,0:T(8,128)(2,1)}, bf16[2048,1024]{1,0:T(8,128)(2,1)}) custom-call(bf16[2048,1024]{1,0:T(8,128)(2,1)} %get-tuple-element.30.att_ref, bf16[2,1,1024,1024]{3,2,1,0:T(8,128)(2,1)} %tok_ref.5, bf16[2,1,1024,1024]{3,2,1,0:T(8,128)(2,1)} %cot_ref.1, bf16[1024,1024]{1,0:T(8,128)(2,1)} %wa_ref.1, ...), custom_call_target="tpu_custom_call" | custom-call | tf_op jit(solution)/shard_map/feed_forward/pallas_call | solution.py:462
  137.9 26.9 %attention_grad.1 = (bf16[2048,1024]{1,0:T(8,128)(2,1)}, bf16[2048,1024]{1,0:T(8,128)(2,1)}, bf16[2048,1024]{1,0:T(8,128)(2,1)}, f32[64,1024]{1,0:T(8,128)}, f32[64,1024]{1,0:T(8,128)}) custom-call(bf16[2048,3072]{1,0:T(8,128)(2,1)} %get-tuple-element.28.q_ref.k_ref.v_ref, bf16[2048,3072]{1,0:T(8,128)(2,1)} %get-tuple-element.28.q_ref.k_ref.v_ref, ...), custom_call_target="tpu_custom_call" | custom-call | tf_op jit(solution)/shard_map/attention_grad/pallas_call | solution.py:565
  164.8 28.6 %grad_first_sum.1 = (bf16[2048,1024]{1,0:T(8,128)(2,1)}, bf16[16,2048]{1,0:T(8,128)(2,1)}) custom-call(bf16[2048,1024]{1,0:T(8,128)(2,1)} %get-tuple-element.34.dq_ref, bf16[2048,1024]{1,0:T(8,128)(2,1)} %get-tuple-element.35.dk_ref, bf16[2048,1024]{1,0:T(8,128)(2,1)} %get-tuple-element.36.dv_ref, bf16[2,1,1024,1024]{3,2,1,0:T(8,128)(2,1)} %tok_ref.5, ...), custom_call_target="tpu_custom_call" | custom-call | tf_op jit(solution)/shard_map/grad_first_sum/pallas_call | solution.py:723
  193.5 8.3 %grad_last.1 = (bf16[2,1,1024,1024]{3,2,1,0:T(8,128)(2,1)}, f32[10,1,1024]{2,1,0:T(1,128)}, f32[1,1024,512]{2,1,0:T(8,128)}, f32[1,512]{1,0:T(1,128)}, f32[1,512,2048]{2,1,0:T(8,128)}, /*index=5*/f32[1,2048]{1,0:T(1,128)}) custom-call(bf16[2048,1024]{1,0:T(8,128)(2,1)} %get-tuple-element.40.grad_hbm, bf16[16,2048]{1,0:T(8,128)(2,1)} %get-tuple-element.41.summed_ref, ...), custom_call_target="tpu_custom_call" | custom-call | tf_op jit(solution)/shard_map/grad_last/pallas_call | solution.py:823

commit v3 on v2

--- a/solution.py
+++ b/solution.py
@@ -92,24 +92,20 @@
     bin_ref,
     wout_hbm,
     bout_ref,
-    *refs,
+    mixed_ref,
+    hidden_ref,
+    states_ref,
+    win,
+    wout,
+    padded,
+    own,
+    gathered,
+    w_ref,
+    current,
+    load_sem,
+    send_sem,
+    recv_sem,
 ):
-    count = (len(refs) - 13) // 2
-    weights_hbm = refs[:count]
-    mixed_ref, hidden_ref, states_ref = refs[count : count + 3]
-    weights = refs[count + 3 : 2 * count + 3]
-    (
-        win,
-        wout,
-        padded,
-        own,
-        gathered,
-        w_ref,
-        current,
-        load_sem,
-        send_sem,
-        recv_sem,
-    ) = refs[2 * count + 3 :]
     step = pl.program_id(0)
     last = pl.num_programs(0) - 1
     row_axis = lax.axis_index("batch")
@@ -118,8 +114,9 @@
 
     width = tok_ref.shape[1]
 
-    copies = [(w_hbm, w_ref), (win_hbm.at[0], win), (wout_hbm.at[0], wout)]
-    copies += list(zip(weights_hbm, weights))
+    columns = [slice(part * width, (part + 1) * width) for part in range(3)]
+    copies = [(w_hbm.at[:, part], w_ref.at[:, part]) for part in columns]
+    copies += [(win_hbm.at[0], win), (wout_hbm.at[0], wout)]
 
     def load(index):
         return pltpu.make_async_copy(*copies[index], load_sem.at[index])
@@ -140,17 +137,15 @@
 
     @pl.when(step == 0)
     def _():
-        load(0).start()
+        for index in range(len(copies)):
+            load(index).start()
         barrier_with(peers)
         current[...] = norm()
-        load(0).wait()
-        for index in range(1, len(copies)):
-            load(index).start()
 
     @pl.when(step == 2)
     def _():
-        load(1).wait()
-        load(2).wait()
+        load(3).wait()
+        load(4).wait()
         padded[...] = jnp.zeros(padded.shape, f32)
         padded[: embed_ref.shape[1], :] = embed_ref[0].astype(f32)
         pre = dot_nn(padded[...].astype(bf16), win[...]) + bin_ref[...].astype(f32)
@@ -164,24 +159,32 @@
         for k in range(1, tasks):
             send(k).start()
 
-    @pl.when(step > 0)
-    def _():
-        mixed = dot_nn(current[...], w_ref[...]) + row_vector(b_ref)
+    def work(ready):
         following = norm()
-        mixed_ref[:, :width] = (mixed[:, :width] * (HEAD_DIM ** (-0.5) * LOG2E)).astype(bf16)
-        mixed_ref[:, width:] = mixed[:, width:].astype(bf16)
+        for index, part in enumerate(columns):
+            ready(index)
+            mixed = dot_nn(current[...], w_ref[:, part]) + row_vector(b_ref, part)
+            if index == 0:
+                mixed = mixed * (HEAD_DIM ** (-0.5) * LOG2E)
+            mixed_ref[:, part] = mixed.astype(bf16)
         current[...] = following
+
+    @pl.when(step == 1)
+    def _():
+        work(lambda index: load(index).wait())
+
+    @pl.when(step > 1)
+    def _():
+        work(lambda index: None)
 
     @pl.when(step == last)
     def _():
         for k in range(1, tasks):
             send(k).wait()
         states_ref[...] = gathered[...].reshape(states_ref.shape)
-        for index in range(3, len(copies)):
-            load(index).wait()
-
-
-def qkv_call(tasks, tokens, gain, shift, w_qkv, b_qkv, embed, w_in, b_in, w_out, b_out, keep):
+
+
+def qkv_call(tasks, tokens, gain, shift, w_qkv, b_qkv, embed, w_in, b_in, w_out, b_out):
     micro, rows, seq, width = tokens.shape
     tile = QKV_TILE
     per_row = seq // tile
@@ -211,20 +214,17 @@
             whole1(b_in),
             pl.BlockSpec(memory_space=pl.ANY),
             whole1(b_out),
-        ]
-        + [pl.BlockSpec(memory_space=pl.ANY)] * len(keep),
+        ],
         out_specs=[
             pl.BlockSpec((tile, 3 * width), lambda i: (jnp.maximum(i - 1, 0), 0)),
             pl.BlockSpec((PAD, rank), lambda i: (0, 0)),
             pl.BlockSpec((tasks * PAD, 2 * width), lambda i: (0, 0)),
-        ]
-        + [pl.BlockSpec(memory_space=pltpu.VMEM)] * len(keep),
+        ],
         out_shape=[
             jax.ShapeDtypeStruct((micro * rows * seq, 3 * width), bf16),
             jax.ShapeDtypeStruct((PAD, rank), f32),
             jax.ShapeDtypeStruct((tasks * PAD, 2 * width), bf16),
-        ]
-        + [pltpu.VMEM(x.shape, bf16) for x in keep],
+        ],
         scratch_shapes=[
             pltpu.VMEM(w_in.shape[1:], bf16),
             pltpu.VMEM(w_out.shape[1:], bf16),
@@ -233,7 +233,7 @@
             pltpu.VMEM((tasks, PAD, 2 * width), bf16),
             pltpu.VMEM(w_qkv.shape, bf16),
             pltpu.VMEM((tile, width), bf16),
-            pltpu.SemaphoreType.DMA((3 + len(keep),)),
+            pltpu.SemaphoreType.DMA((5,)),
             pltpu.SemaphoreType.DMA((tasks - 1,)),
             pltpu.SemaphoreType.DMA((tasks - 1,)),
         ],
@@ -241,7 +241,7 @@
             collective_id=0, has_side_effects=True, vmem_limit_bytes=VMEM_LIMIT
         ),
         name="norm_qkv",
-    )(tokens, gain, shift, w_qkv, b_qkv, embed, w_in, b_in, w_out, b_out, *keep)
+    )(tokens, gain, shift, w_qkv, b_qkv, embed, w_in, b_in, w_out, b_out)
 
 
 def stack_heads(block):
@@ -304,8 +304,9 @@
                 stage(step - delay, *items[step - delay])
 
 
-def attention_kernel(
+def attention_feed_kernel(
     prefix,
+    units,
     task_ref,
     seg_ref,
     q_ref,
@@ -313,25 +314,61 @@
     v_ref,
     pk_ref,
     pv_ref,
-    *refs,
+    tok_ref,
+    cot_ref,
+    wa_hbm,
+    ba_ref,
+    gain_ref,
+    shift_ref,
+    wf_hbm,
+    bf_ref,
+    wp_hbm,
+    bp_ref,
+    probs_ref,
+    out_ref,
+    gres_ref,
+    gatt_ref,
+    bias,
+    by_key,
+    work,
+    attended,
+    act_all,
+    gpre_all,
+    wa_ref,
+    wf_ref,
+    wp_ref,
+    weight_sem,
 ):
-    out_ref, probs_ref, bias, by_key, work = refs
-    micro = pl.program_id(0)
-
-    @pl.when(pl.program_id(1) == 0)
+    step = pl.program_id(0)
+    groups = attended.shape[1]
+    unit = jnp.minimum(step, units - 1)
+    micro = unit // groups
+    group = lax.rem(unit, groups)
+    loads = [
+        pltpu.make_async_copy(source, target, weight_sem.at[index])
+        for index, (source, target) in enumerate(
+            ((wa_hbm, wa_ref), (wf_hbm, wf_ref), (wp_hbm, wp_ref))
+        )
+    ]
+
+    for index in range(len(loads)):
+
+        @pl.when(step == 1 + 2 * index)
+        def _():
+            loads[index].start()
+
+    @pl.when((step < units) & (group == 0))
     def _():
         fill_mask(seg_ref, task_ref, micro, prefix, bias, by_key)
 
-    height = work.shape[1]
-    pieces = [slice(c, c + CHUNK) for c in range(0, height, CHUNK)]
-
-    def scores(index, group, block):
-        lanes = slice(group * LANES, (group + 1) * LANES)
-        keys = jnp.concatenate([k_ref[own_window(block), lanes], pk_ref[:, lanes]], axis=0)
-        queries = stack_heads(q_ref[block * QB : (block + 1) * QB, lanes])
+    pieces = [slice(c, c + CHUNK) for c in range(0, work.shape[1], CHUNK)]
+
+    def scores(index, block):
+        keys = jnp.concatenate([k_ref[own_window(block), :], pk_ref[...]], axis=0)
+        queries = stack_heads(q_ref[block * QB : (block + 1) * QB, :])
         work[index % 2] = dot_nt(keys, queries)
 
-    def softmax(index, group, block):
+    def softmax(index, block):
         slot = work.at[index % 2]
         top = None
         for piece in pieces:
@@ -349,130 +386,127 @@
             total = part if total is None else total + part
         inverse = 1.0 / jnp.sum(total, axis=0, keepdims=True)
         for piece in pieces:
-            probs_ref[group, block, piece, :] = (slot[piece, :] * inverse).astype(bf16)
-
-    def attend(index, group, block):
-        lanes = slice(group * LANES, (group + 1) * LANES)
-        values = jnp.concatenate([v_ref[own_window(block), lanes], pv_ref[:, lanes]], axis=0)
-        result = pick_heads(dot_tn(probs_ref[group, block], values))
-        out_ref[block * QB : (block + 1) * QB, lanes] = result.astype(bf16)
-
-    items = [
-        (group, block)
-        for group in range(q_ref.shape[1] // LANES)
-        for block in range(q_ref.shape[0] // QB)
-    ]
-    skewed(items, scores, softmax, attend)
-
-
-def attention_call(mixed, segments, tasks, states, prefix):
-    micro, _, seq = segments.shape
-    width = mixed.shape[1] // 3
+            probs_ref[block, piece, :] = (slot[piece, :] * inverse).astype(bf16)
+
+    def attend(index, block):
+        values = jnp.concatenate([v_ref[own_window(block), :], pv_ref[...]], axis=0)
+        result = pick_heads(dot_tn(probs_ref[block], values))
+        attended[micro, group, block * QB : (block + 1) * QB, :] = result.astype(bf16)
+
+    @pl.when(step < units)
+    def _():
+        blocks = [(block,) for block in range(q_ref.shape[0] // QB)]
+        skewed(blocks, scores, softmax, attend)
+
+    @pl.when(step == units)
+    def _():
+        for load in loads:
+            load.wait()
+
+    @pl.when(step >= units)
+    def _():
+        tile = tok_ref.shape[0]
+        per_row = attended.shape[2] // tile
+        index = jnp.maximum(step - units, 0)
+        rows = pl.ds(pl.multiple_of(lax.rem(index, per_row) * tile, tile), tile)
+        tile_attended = jnp.concatenate(
+            [attended[index // per_row, g, rows, :] for g in range(groups)], axis=1
+        )
+        gain = row_vector(gain_ref)
+        resid = tok_ref[...].astype(f32) + dot_nn(tile_attended, wa_ref[...]) + row_vector(ba_ref)
+        unit_norm, inverse = normalise(resid)
+        normed = (unit_norm * gain + row_vector(shift_ref)).astype(bf16)
+        grad_out = cot_ref[...]
+        for start in range(0, wf_ref.shape[1], FF_CHUNK):
+            part = slice(start, start + FF_CHUNK)
+            pre = dot_nn(normed, wf_ref[:, part]) + row_vector(bf_ref, part)
+            act, gpre = gelu_both(pre, dot_nt(grad_out, wp_ref[part, :]))
+            act_all[:, part] = act
+            gpre_all[:, part] = gpre
+        grad_normed = dot_nt(gpre_all[...], wf_ref[...])
+        out = resid + dot_nn(act_all[...], wp_ref[...]) + row_vector(bp_ref)
+        out_ref[...] = out.astype(bf16)
+        grad_resid = grad_out.astype(f32) + norm_backward(grad_normed, gain, unit_norm, inverse)
+        grad_branch = grad_resid.astype(bf16)
+        gres_ref[...] = grad_branch
+        gatt_ref[...] = dot_nt(grad_branch, wa_ref[...]).astype(bf16)
+
+
+def attention_feed_call(
+    mixed, segments, tasks, states, prefix, tokens, cotangent, weights
+):
+    micro, _, seq, width = tokens.shape
     groups = width // LANES
     blocks = seq // QB
-    keys = WIN + states.shape[0]
-    both = 2
-    steps = groups // both
-    part = lambda offset: pl.BlockSpec((seq, both * LANES), lambda r, g: (r, offset + g))
+    prefix_rows = states.shape[0]
+    keys = WIN + prefix_rows
+    units = micro * groups
+    tile = 256
+    per_row = seq // tile
+    count = micro * seq
+    w_attn, _, _, _, w_fc, _, w_proj, _ = weights
+    unit = lambda i: jnp.minimum(i, units - 1)
+    index = lambda i: jnp.maximum(i - units, 0)
+    part = lambda offset: pl.BlockSpec(
+        (seq, LANES), lambda i: (unit(i) // groups, offset + lax.rem(unit(i), groups))
+    )
     piece = lambda offset: pl.BlockSpec(
-        (states.shape[0], both * LANES), lambda r, g: (0, offset + g)
-    )
+        (prefix_rows, LANES), lambda i: (0, offset + lax.rem(unit(i), groups))
+    )
+    flat = pl.BlockSpec((tile, width), lambda i: (index(i), 0))
+    deep = pl.BlockSpec(
+        (None, None, tile, width),
+        lambda i: (index(i) // per_row, 0, lax.rem(index(i), per_row), 0),
+    )
+
+    def weight(x):
+        if x.ndim == 2:
+            return pl.BlockSpec(memory_space=pl.ANY)
+        return pl.BlockSpec(x.shape, lambda i: (0,))
+
     return pl.pallas_call(
-        functools.partial(attention_kernel, prefix),
-        grid=(micro, steps),
+        functools.partial(attention_feed_kernel, prefix, units),
+        grid=(units + count // tile,),
         in_specs=[
             pl.BlockSpec(memory_space=pltpu.SMEM),
-            pl.BlockSpec((None, 1, seq), lambda r, g: (r, 0, 0)),
+            pl.BlockSpec((None, 1, seq), lambda i: (unit(i) // groups, 0, 0)),
             part(0),
-            part(steps),
-            part(2 * steps),
+            part(groups),
+            part(2 * groups),
             piece(0),
-            piece(steps),
-        ],
+            piece(groups),
+            deep,
+            deep,
+        ]
+        + [weight(x) for x in weights],
         out_specs=[
-            part(0),
-            pl.BlockSpec((None, both, blocks, keys, LANES), lambda r, g: (r, g, 0, 0, 0)),
+            pl.BlockSpec(
+                (None, None, blocks, keys, LANES),
+                lambda i: (unit(i) // groups, lax.rem(unit(i), groups), 0, 0, 0),
+            ),
+            deep,
+            flat,
+            flat,
         ],
         out_shape=[
-            jax.ShapeDtypeStruct((micro * seq, width), bf16),
             jax.ShapeDtypeStruct((micro, groups, blocks, keys, LANES), bf16),
+            jax.ShapeDtypeStruct(tokens.shape, bf16),
+            jax.ShapeDtypeStruct((count, width), bf16),
+            jax.ShapeDtypeStruct((count, width), bf16),
         ],
         scratch_shapes=[
             pltpu.VMEM((blocks, keys, 128), f32),
             pltpu.VMEM((seq, 128), f32),
             pltpu.VMEM((2, keys, LANES), f32),
-        ],
+            pltpu.VMEM((micro, groups, seq, LANES), bf16),
+            pltpu.VMEM((tile, w_fc.shape[1]), bf16),
+            pltpu.VMEM((tile, w_fc.shape[1]), bf16),
+        ]
+        + [pltpu.VMEM(x.shape, bf16) for x in (w_attn, w_fc, w_proj)]
+        + [pltpu.SemaphoreType.DMA((3,))],
         compiler_params=pltpu.CompilerParams(vmem_limit_bytes=VMEM_LIMIT),
-        name="attention",
-    )(tasks, segments, mixed, mixed, mixed, states, states)
-
-
-def mlp_kernel(
-    att_ref,
-    tok_ref,
-    cot_ref,
-    wa_ref,
-    ba_ref,
-    gain_ref,
-    shift_ref,
-    wf_ref,
-    bf_ref,
-    wp_ref,
-    bp_ref,
-    out_ref,
-    gres_ref,
-    gatt_ref,
-    act_all,
-    gpre_all,
-):
-    gain = row_vector(gain_ref)
-    resid = tok_ref[...].astype(f32) + dot_nn(att_ref[...], wa_ref[...]) + row_vector(ba_ref)
-    unit, inverse = normalise(resid)
-    normed = (unit * gain + row_vector(shift_ref)).astype(bf16)
-    grad_out = cot_ref[...]
-    for start in range(0, wf_ref.shape[1], FF_CHUNK):
-        part = slice(start, start + FF_CHUNK)
-        pre = dot_nn(normed, wf_ref[:, part]) + row_vector(bf_ref, part)
-        act, gpre = gelu_both(pre, dot_nt(grad_out, wp_ref[part, :]))
-        act_all[:, part] = act
-        gpre_all[:, part] = gpre
-    grad_normed = dot_nt(gpre_all[...], wf_ref[...])
-    out = resid + dot_nn(act_all[...], wp_ref[...]) + row_vector(bp_ref)
-    out_ref[...] = out.astype(bf16)
-    grad_resid = grad_out.astype(f32) + norm_backward(grad_normed, gain, unit, inverse)
-    grad_branch = grad_resid.astype(bf16)
-    gres_ref[...] = grad_branch
-    gatt_ref[...] = dot_nt(grad_branch, wa_ref[...]).astype(bf16)
-
-
-def mlp_call(attended, tokens, cotangent, w_attn, b_attn, gain, shift, w_fc, b_fc, w_proj, b_proj):
-    micro, rows, seq, width = tokens.shape
-    tile = 256
-    per_row = seq // tile
-    flat = pl.BlockSpec((tile, width), lambda i: (i, 0))
-    deep = pl.BlockSpec(
-        (None, None, tile, width),
-        lambda i: (i // (rows * per_row), (i // per_row) % rows, i % per_row, 0),
-    )
-    once = lambda x: pl.BlockSpec(
-        x.shape, lambda i: (0,) * x.ndim, pipeline_mode=pl.Buffered(1)
-    )
-    weights = (w_attn, b_attn, gain, shift, w_fc, b_fc, w_proj, b_proj)
-    count = micro * rows * seq
-    return pl.pallas_call(
-        mlp_kernel,
-        grid=(count // tile,),
-        in_specs=[flat, deep, deep] + [once(x) for x in weights],
-        out_specs=[deep, flat, flat],
-        out_shape=[
-            jax.ShapeDtypeStruct(tokens.shape, bf16),
-            jax.ShapeDtypeStruct((count, width), bf16),
-            jax.ShapeDtypeStruct((count, width), bf16),
-        ],
-        scratch_shapes=[pltpu.VMEM((tile, w_fc.shape[1]), bf16)] * 2,
-        compiler_params=pltpu.CompilerParams(vmem_limit_bytes=VMEM_LIMIT),
-        name="feed_forward",
-    )(attended, tokens, cotangent, *weights)
+        name="attention_feed",
+    )(tasks, segments, mixed, mixed, mixed, states, states, tokens, cotangent, *weights)
 
 
 def attention_grad_kernel(
@@ -617,7 +651,14 @@
     shard_peers = [(lax.rem(shard + k, shards), task) for k in range(1, shards)]
     width = dpk_ref.shape[1]
     lanes = send_b.shape[2]
-    load = pltpu.make_async_copy(w_hbm, w_ref, load_sem)
+    loads = [
+        pltpu.make_async_copy(
+            w_hbm.at[:, index * width : (index + 1) * width],
+            w_ref.at[:, index * width : (index + 1) * width],
+            load_sem.at[index],
+        )
+        for index in range(3)
+    ]
 
     def to_task(k):
         return pltpu.make_async_remote_copy(
@@ -678,13 +719,13 @@
 
     @pl.when(step == 0)
     def _():
-        load.start()
+        for load in loads:
+            load.start()
         barrier_with(task_peers + shard_peers)
         for t in range(tasks):
             part = slice(t * PAD, (t + 1) * PAD)
             send_a[t, :, :width] = dpk_ref[part, :].astype(bf16)
             send_a[t, :, width:] = dpv_ref[part, :].astype(bf16)
-        load.wait()
 
     @pl.when(step == 1)
     def _():
@@ -698,12 +739,22 @@
     def _():
         start_back()
 
-    grad = dot_nt(dq_ref[...], w_ref[:, :width])
-    grad = grad + dot_nt(dk_ref[...], w_ref[:, width : 2 * width])
-    grad = grad + dot_nt(dv_ref[...], w_ref[:, 2 * width :])
-    unit, inverse = normalise(tok_ref[...].astype(f32))
-    back = norm_backward(grad, row_vector(gain_ref), unit, inverse)
-    grad_ref[...] = (gres_ref[...].astype(f32) + back).astype(bf16)
+    def work(ready):
+        grad = 0.0
+        for index, part in enumerate((dq_ref, dk_ref, dv_ref)):
+            ready(index)
+            grad = grad + dot_nt(part[...], w_ref[:, index * width : (index + 1) * width])
+        unit, inverse = normalise(tok_ref[...].astype(f32))
+        back = norm_backward(grad, row_vector(gain_ref), unit, inverse)
+        grad_ref[...] = (gres_ref[...].astype(f32) + back).astype(bf16)
+
+    @pl.when(step == 0)
+    def _():
+        work(lambda index: loads[index].wait())
+
+    @pl.when(step > 0)
+    def _():
+        work(lambda index: None)
 
     @pl.when(step == last)
     def _():
@@ -744,7 +795,7 @@
             pltpu.VMEM((shards, PAD, lanes), bf16),
             pltpu.VMEM((shards - 1, PAD, lanes), bf16),
             pltpu.VMEM((shards, PAD, lanes), bf16),
-            pltpu.SemaphoreType.DMA,
+            pltpu.SemaphoreType.DMA((3,)),
             pltpu.SemaphoreType.DMA((2, tasks - 1)),
             pltpu.SemaphoreType.DMA((4, shards - 1)),
         ],
@@ -881,7 +932,7 @@
     reparam_out,
     reparam_out_bias,
 ):
-    mixed, hidden, states, *kept = qkv_call(
+    mixed, hidden, states = qkv_call(
         tasks,
         tokens,
         ln1_gain,
@@ -893,23 +944,16 @@
         reparam_in_bias,
         reparam_out,
         reparam_out_bias,
-        (),
-    )
-    attended, probs = attention_call(
-        mixed, segment_ids, task_ids, states, prefix_embed.shape[1]
-    )
-    block_out, grad_resid, grad_attended = mlp_call(
-        attended,
+    )
+    probs, block_out, grad_resid, grad_attended = attention_feed_call(
+        mixed,
+        segment_ids,
+        task_ids,
+        states,
+        prefix_embed.shape[1],
         tokens,
         cotangent,
-        w_attn_out,
-        b_attn_out,
-        ln2_gain,
-        ln2_bias,
-        w_fc,
-        b_fc,
-        w_proj,
-        b_proj,
+        (w_attn_out, b_attn_out, ln2_gain, ln2_bias, w_fc, b_fc, w_proj, b_proj),
     )
     dq, dk, dv, dpk, dpv = attention_grad_call(mixed, states, probs, grad_attended)
     tile = 512

time: 202 us -> 199 us (0.985)
  Pallas kernels: 201 us -> 198 us
    pallas_call x2 -> x1, Pallas kernels: 116 us -> 113 us  [attention_feed_call(): pl.pallas_call(functools.partial(attention_feed_kernel, prefix, units), g...]
where the time goes in v3:
time: 199 us; the launch traced here: 198 us
  Pallas kernels  198 us (99%)
    pallas_call x1, Pallas kernels, attention_feed_call(): pl.pallas_call(functools.partial(attention_feed_kernel, prefix, units), g...  113 us
    pallas_call x1, Pallas kernels, sum_call(): pl.pallas_call(functools.partial(sum_kernel, tasks, shards), grid=(tiles,...  28.4 us
    pallas_call x1, Pallas kernels, attention_grad_call(): pl.pallas_call(attention_grad_kernel, grid=(groups, micro), in_specs=[par...  26.7 us
    pallas_call x1, Pallas kernels, qkv_call(): pl.pallas_call(functools.partial(qkv_kernel, tasks), grid=(tiles + 1,), i...  20.8 us
    pallas_call x1, Pallas kernels, last_call(): pl.pallas_call(last_kernel, grid=(1,), in_specs=[anywhere] + [whole(x.sha...  8.31 us

profile of v3, /device:TPU:0, one launch (start us, length us, event | category | flops | bytes accessed | tf_op | source)
XLA Modules:
  0.0 198.4 jit_solution(16613995613334840501)
XLA Ops:
  0.6 20.8 %norm_qkv.1 = (bf16[2048,3072]{1,0:T(8,128)(2,1)}, f32[16,512]{1,0:T(8,128)}, bf16[64,2048]{1,0:T(8,128)(2,1)}) custom-call(bf16[2,1,1024,1024]{3,2,1,0:T(8,128)(2,1)} %tok_ref.5, bf16[1024]{0:T(1024)(128)(2,1)} %gain_ref.5, bf16[1024]{0:T(1024)(128)(2,1)} %shift_ref.2, bf16[1024,3072]{1,0:T(8,128)(2,1)} %w_hbm.3, bf16[3072]{0:T(1024)(128)(2,1)} %b_ref.1, ...), custom_call_target="tpu_custom_call" | custom-call | tf_op jit(solution)/shard_map/norm_qkv/pallas_call | solution.py:195
  21.5 113.4 %attention_feed.1 = (bf16[2,4,16,256,256]{4,3,2,1,0:T(8,128)(2,1)}, bf16[2,1,1024,1024]{3,2,1,0:T(8,128)(2,1)}, bf16[2048,1024]{1,0:T(8,128)(2,1)}, bf16[2048,1024]{1,0:T(8,128)(2,1)}) custom-call(s32[2,1,16]{2,1,0:T(1,128)} %task_ref.1, s32[2,1,1024]{2,1,0:T(1,128)} %seg_ref.1, bf16[2048,3072]{1,0:T(8,128)(2,1)} %get-tuple-element.27.q_ref.k_ref.v_ref, ...), custom_call_target="tpu_custom_call" | custom-call | tf_op jit(solution)/shard_map/attention_feed/pallas_call | solution.py:467
  134.8 26.7 %attention_grad.1 = (bf16[2048,1024]{1,0:T(8,128)(2,1)}, bf16[2048,1024]{1,0:T(8,128)(2,1)}, bf16[2048,1024]{1,0:T(8,128)(2,1)}, f32[64,1024]{1,0:T(8,128)}, f32[64,1024]{1,0:T(8,128)}) custom-call(bf16[2048,3072]{1,0:T(8,128)(2,1)} %get-tuple-element.27.q_ref.k_ref.v_ref, bf16[2048,3072]{1,0:T(8,128)(2,1)} %get-tuple-element.27.q_ref.k_ref.v_ref, ...), custom_call_target="tpu_custom_call" | custom-call | tf_op jit(solution)/shard_map/attention_grad/pallas_call | solution.py:599
  161.5 28.4 %grad_first_sum.1 = (bf16[2048,1024]{1,0:T(8,128)(2,1)}, bf16[16,2048]{1,0:T(8,128)(2,1)}) custom-call(bf16[2048,1024]{1,0:T(8,128)(2,1)} %get-tuple-element.32.dq_ref, bf16[2048,1024]{1,0:T(8,128)(2,1)} %get-tuple-element.33.dk_ref, bf16[2048,1024]{1,0:T(8,128)(2,1)} %get-tuple-element.34.dv_ref, bf16[2,1,1024,1024]{3,2,1,0:T(8,128)(2,1)} %tok_ref.5, ...), custom_call_target="tpu_custom_call" | custom-call | tf_op jit(solution)/shard_map/grad_first_sum/pallas_call | solution.py:774
  189.9 8.3 %grad_last.1 = (bf16[2,1,1024,1024]{3,2,1,0:T(8,128)(2,1)}, f32[10,1,1024]{2,1,0:T(1,128)}, f32[1,1024,512]{2,1,0:T(8,128)}, f32[1,512]{1,0:T(1,128)}, f32[1,512,2048]{2,1,0:T(8,128)}, /*index=5*/f32[1,2048]{1,0:T(1,128)}) custom-call(bf16[2048,1024]{1,0:T(8,128)(2,1)} %get-tuple-element.38.grad_hbm, bf16[16,2048]{1,0:T(8,128)(2,1)} %get-tuple-element.39.summed_ref, ...), custom_call_target="tpu_custom_call" | custom-call | tf_op jit(solution)/shard_map/grad_last/pallas_call | solution.py:874

commit v4 on v3

--- a/solution.py
+++ b/solution.py
@@ -353,7 +353,7 @@
 
     for index in range(len(loads)):
 
-        @pl.when(step == 1 + 2 * index)
+        @pl.when(step == index)
         def _():
             loads[index].start()
 
@@ -363,12 +363,13 @@
 
     pieces = [slice(c, c + CHUNK) for c in range(0, work.shape[1], CHUNK)]
 
-    def scores(index, block):
-        keys = jnp.concatenate([k_ref[own_window(block), :], pk_ref[...]], axis=0)
-        queries = stack_heads(q_ref[block * QB : (block + 1) * QB, :])
+    def scores(index, half, block):
+        lanes = slice(half * LANES, (half + 1) * LANES)
+        keys = jnp.concatenate([k_ref[own_window(block), lanes], pk_ref[:, lanes]], axis=0)
+        queries = stack_heads(q_ref[block * QB : (block + 1) * QB, lanes])
         work[index % 2] = dot_nt(keys, queries)
 
-    def softmax(index, block):
+    def softmax(index, half, block):
         slot = work.at[index % 2]
         top = None
         for piece in pieces:
@@ -386,17 +387,22 @@
             total = part if total is None else total + part
         inverse = 1.0 / jnp.sum(total, axis=0, keepdims=True)
         for piece in pieces:
-            probs_ref[block, piece, :] = (slot[piece, :] * inverse).astype(bf16)
-
-    def attend(index, block):
-        values = jnp.concatenate([v_ref[own_window(block), :], pv_ref[...]], axis=0)
-        result = pick_heads(dot_tn(probs_ref[block], values))
-        attended[micro, group, block * QB : (block + 1) * QB, :] = result.astype(bf16)
+            probs_ref[half, block, piece, :] = (slot[piece, :] * inverse).astype(bf16)
+
+    def attend(index, half, block):
+        lanes = slice(half * LANES, (half + 1) * LANES)
+        values = jnp.concatenate([v_ref[own_window(block), lanes], pv_ref[:, lanes]], axis=0)
+        result = pick_heads(dot_tn(probs_ref[half, block], values))
+        attended[micro, group, block * QB : (block + 1) * QB, lanes] = result.astype(bf16)
 
     @pl.when(step < units)
     def _():
-        blocks = [(block,) for block in range(q_ref.shape[0] // QB)]
-        skewed(blocks, scores, softmax, attend)
+        items = [
+            (half, block)
+            for half in range(q_ref.shape[1] // LANES)
+            for block in range(q_ref.shape[0] // QB)
+        ]
+        skewed(items, scores, softmax, attend)
 
     @pl.when(step == units)
     def _():
@@ -440,7 +446,9 @@
     blocks = seq // QB
     prefix_rows = states.shape[0]
     keys = WIN + prefix_rows
-    units = micro * groups
+    both = 2
+    steps = groups // both
+    units = micro * steps
     tile = 256
     per_row = seq // tile
     count = micro * seq
@@ -448,10 +456,10 @@
     unit = lambda i: jnp.minimum(i, units - 1)
     index = lambda i: jnp.maximum(i - units, 0)
     part = lambda offset: pl.BlockSpec(
-        (seq, LANES), lambda i: (unit(i) // groups, offset + lax.rem(unit(i), groups))
+        (seq, both * LANES), lambda i: (unit(i) // steps, offset + lax.rem(unit(i), steps))
     )
     piece = lambda offset: pl.BlockSpec(
-        (prefix_rows, LANES), lambda i: (0, offset + lax.rem(unit(i), groups))
+        (prefix_rows, both * LANES), lambda i: (0, offset + lax.rem(unit(i), steps))
     )
     flat = pl.BlockSpec((tile, width), lambda i: (index(i), 0))
     deep = pl.BlockSpec(
@@ -469,20 +477,20 @@
         grid=(units + count // tile,),
         in_specs=[
             pl.BlockSpec(memory_space=pltpu.SMEM),
-            pl.BlockSpec((None, 1, seq), lambda i: (unit(i) // groups, 0, 0)),
+            pl.BlockSpec((None, 1, seq), lambda i: (unit(i) // steps, 0, 0)),
             part(0),
-            part(groups),
-            part(2 * groups),
+            part(steps),
+            part(2 * steps),
             piece(0),
-            piece(groups),
+            piece(steps),
             deep,
             deep,
         ]
         + [weight(x) for x in weights],
         out_specs=[
             pl.BlockSpec(
-                (None, None, blocks, keys, LANES),
-                lambda i: (unit(i) // groups, lax.rem(unit(i), groups), 0, 0, 0),
+                (None, both, blocks, keys, LANES),
+                lambda i: (unit(i) // steps, lax.rem(unit(i), steps), 0, 0, 0),
             ),
             deep,
             flat,
@@ -498,7 +506,7 @@
             pltpu.VMEM((blocks, keys, 128), f32),
             pltpu.VMEM((seq, 128), f32),
             pltpu.VMEM((2, keys, LANES), f32),
-            pltpu.VMEM((micro, groups, seq, LANES), bf16),
+            pltpu.VMEM((micro, steps, seq, both * LANES), bf16),
             pltpu.VMEM((tile, w_fc.shape[1]), bf16),
             pltpu.VMEM((tile, w_fc.shape[1]), bf16),
         ]

time: 199 us -> 196 us (0.985)
  Pallas kernels: 198 us -> 195 us
    pallas_call x1, Pallas kernels: 113 us -> 111 us  [attention_feed_call(): pl.pallas_call(functools.partial(attention_feed_kernel, prefix, units), g...]
where the time goes in v4:
time: 196 us
  Pallas kernels  195 us (99%)
    pallas_call x1, Pallas kernels, attention_feed_call(): pl.pallas_call(functools.partial(attention_feed_kernel, prefix, units), g...  111 us
    pallas_call x1, Pallas kernels, sum_call(): pl.pallas_call(functools.partial(sum_kernel, tasks, shards), grid=(tiles,...  28.3 us
    pallas_call x1, Pallas kernels, attention_grad_call(): pl.pallas_call(attention_grad_kernel, grid=(groups, micro), in_specs=[par...  26.7 us
    pallas_call x1, Pallas kernels, qkv_call(): pl.pallas_call(functools.partial(qkv_kernel, tasks), grid=(tiles + 1,), i...  20.8 us
    pallas_call x1, Pallas kernels, last_call(): pl.pallas_call(last_kernel, grid=(1,), in_specs=[anywhere] + [whole(x.sha...  8.31 us

profile of v4, /device:TPU:0, one launch (start us, length us, event | category | flops | bytes accessed | tf_op | source)
XLA Modules:
  0.0 195.9 jit_solution(291178522074401663)
XLA Ops:
  0.6 20.8 %norm_qkv.1 = (bf16[2048,3072]{1,0:T(8,128)(2,1)}, f32[16,512]{1,0:T(8,128)}, bf16[64,2048]{1,0:T(8,128)(2,1)}) custom-call(bf16[2,1,1024,1024]{3,2,1,0:T(8,128)(2,1)} %tok_ref.5, bf16[1024]{0:T(1024)(128)(2,1)} %gain_ref.5, bf16[1024]{0:T(1024)(128)(2,1)} %shift_ref.2, bf16[1024,3072]{1,0:T(8,128)(2,1)} %w_hbm.3, bf16[3072]{0:T(1024)(128)(2,1)} %b_ref.1, ...), custom_call_target="tpu_custom_call" | custom-call | tf_op jit(solution)/shard_map/norm_qkv/pallas_call | solution.py:195
  21.5 110.9 %attention_feed.1 = (bf16[2,4,16,256,256]{4,3,2,1,0:T(8,128)(2,1)}, bf16[2,1,1024,1024]{3,2,1,0:T(8,128)(2,1)}, bf16[2048,1024]{1,0:T(8,128)(2,1)}, bf16[2048,1024]{1,0:T(8,128)(2,1)}) custom-call(s32[2,1,16]{2,1,0:T(1,128)} %task_ref.1, s32[2,1,1024]{2,1,0:T(1,128)} %seg_ref.1, bf16[2048,3072]{1,0:T(8,128)(2,1)} %get-tuple-element.27.q_ref.k_ref.v_ref, ...), custom_call_target="tpu_custom_call" | custom-call | tf_op jit(solution)/shard_map/attention_feed/pallas_call | solution.py:475
  132.3 26.7 %attention_grad.1 = (bf16[2048,1024]{1,0:T(8,128)(2,1)}, bf16[2048,1024]{1,0:T(8,128)(2,1)}, bf16[2048,1024]{1,0:T(8,128)(2,1)}, f32[64,1024]{1,0:T(8,128)}, f32[64,1024]{1,0:T(8,128)}) custom-call(bf16[2048,3072]{1,0:T(8,128)(2,1)} %get-tuple-element.27.q_ref.k_ref.v_ref, bf16[2048,3072]{1,0:T(8,128)(2,1)} %get-tuple-element.27.q_ref.k_ref.v_ref, ...), custom_call_target="tpu_custom_call" | custom-call | tf_op jit(solution)/shard_map/attention_grad/pallas_call | solution.py:607
  159.0 28.3 %grad_first_sum.1 = (bf16[2048,1024]{1,0:T(8,128)(2,1)}, bf16[16,2048]{1,0:T(8,128)(2,1)}) custom-call(bf16[2048,1024]{1,0:T(8,128)(2,1)} %get-tuple-element.32.dq_ref, bf16[2048,1024]{1,0:T(8,128)(2,1)} %get-tuple-element.33.dk_ref, bf16[2048,1024]{1,0:T(8,128)(2,1)} %get-tuple-element.34.dv_ref, bf16[2,1,1024,1024]{3,2,1,0:T(8,128)(2,1)} %tok_ref.5, ...), custom_call_target="tpu_custom_call" | custom-call | tf_op jit(solution)/shard_map/grad_first_sum/pallas_call | solution.py:782
  187.4 8.3 %grad_last.1 = (bf16[2,1,1024,1024]{3,2,1,0:T(8,128)(2,1)}, f32[10,1,1024]{2,1,0:T(1,128)}, f32[1,1024,512]{2,1,0:T(8,128)}, f32[1,512]{1,0:T(1,128)}, f32[1,512,2048]{2,1,0:T(8,128)}, /*index=5*/f32[1,2048]{1,0:T(1,128)}) custom-call(bf16[2048,1024]{1,0:T(8,128)(2,1)} %get-tuple-element.38.grad_hbm, bf16[16,2048]{1,0:T(8,128)(2,1)} %get-tuple-element.39.summed_ref, ...), custom_call_target="tpu_custom_call" | custom-call | tf_op jit(solution)/shard_map/grad_last/pallas_call | solution.py:882
